TPU v7x, 512 devices: a whole 4x8x8 slice. The times are simulated.
512 devices in a mesh: row: 32 (over y, x), col: 16 (over z, core).
Axes of the slice: x: 4, y: 8, z: 8, core: 2. Of those that a mesh axis runs over, the one named last changes fastest.
Arguments:
- homolog_representation: bfloat16 [256, 512, 64], P('row', 'col'), may hold values from -1.5 to 1.5
- pair_state: bfloat16 [512, 512, 128], P('row', 'col'), may hold values from -6 to 6
- homolog_present: int32 [256], replicated, may hold values 0 or 1
- token_live_mask: int32 [512], replicated, may hold values 0 or 1
- product_projection: bfloat16 [64, 64], replicated, may hold values from -0.75 to 0.75
- mean_matrix: bfloat16 [1024, 128], replicated, may hold values from -0.75 to 0.75
- score_matrix: float32 [128, 8], replicated, may hold values from -17.5 to 17.5
- payload_projection: bfloat16 [64, 256], replicated, may hold values from -0.75 to 0.75
- switch_projection: bfloat16 [64, 256], replicated, may hold values from -0.75 to 0.75
- return_projection: bfloat16 [256, 64], replicated, may hold values from -1.5 to 1.5
- transition_input: bfloat16 [128, 1024], replicated, may hold values from -0.5 to 0.5
- transition_output: bfloat16 [512, 128], replicated, may hold values from -0.25 to 0.25
Outputs:
- alignment_output: bfloat16 [256, 512, 64], P('row', 'col')
- pair_output: bfloat16 [512, 512, 128], P('row', 'col')
All inputs are finite; a program needn't handle non-finite values.
Results may differ from a plain program's by a relative error of at most 0.038.
Values may be sent and summed in bfloat16 or wider, within the bound.
A program may use at most 64 MiB of HBM per device.

v0:
```python
import jax
import jax.numpy as jnp
from jax import lax
from jax.sharding import Mesh
from jax.sharding import PartitionSpec as P

COL = ("col_0", "col_1")


epsilon = 1e-05


def gather_axes(x, axes, dim):
    whole = x
    for number in range(len(axes) - 1, -1, -1):
        whole = lax.all_gather(whole, axes[number], axis=dim, tiled=True)
    return whole


def from_everyone(x, axis):
    copies = jnp.broadcast_to(x, (lax.axis_size(axis), *x.shape))
    return lax.all_to_all(copies, axis, split_axis=0, concat_axis=0, tiled=True)


def in_order(pieces, dim):
    lengths = list(pieces.shape[1:])
    lengths[dim] *= pieces.shape[0]
    return jnp.moveaxis(pieces, 0, dim).reshape(lengths)


def gathered_copies(x, axis, dim):
    pieces = from_everyone(x, axis)
    return in_order(pieces, dim)


def in_blocks(x, dim, size):
    lengths = x.shape
    pieces = x.reshape(*lengths[:dim], size, lengths[dim] // size, *lengths[dim + 1 :])
    return jnp.moveaxis(pieces, dim, 0)


def sent_and_summed(x, axis, dim):
    pieces = in_blocks(x, dim, lax.axis_size(axis))
    arrived = lax.all_to_all(pieces, axis, split_axis=0, concat_axis=0, tiled=True)
    return arrived.astype(jnp.float32).sum(axis=0)


def normalized_rows(source):
    source = source.astype(jnp.float32)
    center = source - jnp.mean(source, axis=-1, keepdims=True)
    spread = jnp.mean(center * center, axis=-1, keepdims=True)
    return center * lax.rsqrt(spread + epsilon)


def softmax_last(scores):
    row_top = jnp.max(scores, axis=-1, keepdims=True)
    exp_scores = jnp.exp(scores - row_top)
    return (exp_scores / jnp.sum(exp_scores, axis=-1, keepdims=True)).astype(jnp.bfloat16)


def body(
    homolog_representation,
    pair_state,
    homolog_present,
    token_live_mask,
    product_projection,
    mean_matrix,
    score_matrix,
    payload_projection,
    switch_projection,
    return_projection,
    transition_input,
    transition_output,
):
    col_devices = lax.axis_size(COL)
    row_index = lax.axis_index("row")
    col_index = lax.axis_index(COL)
    sequence_count, column_tokens, alignment_width = homolog_representation.shape
    row_tokens, _, pair_width = pair_state.shape
    token_count = column_tokens * col_devices
    outer_channel_width = product_projection.shape[1] // 2
    head_count = score_matrix.shape[1]
    mixed_width = payload_projection.shape[1]
    ff_width = transition_output.shape[0]
    repeats = max(1, col_devices // head_count)
    head_slots = head_count * repeats // col_devices
    piece_width = mixed_width // col_devices
    slot_width = piece_width // head_slots
    complete_alignment = gather_axes(homolog_representation, COL, 1)
    homolog_standardized = (
        normalized_rows(complete_alignment)
        .astype(jnp.bfloat16)
        .reshape(sequence_count * token_count, alignment_width)
    )
    local_norm = (
        normalized_rows(homolog_representation)
        .astype(jnp.bfloat16)
        .reshape(sequence_count * column_tokens, alignment_width)
    )
    seq_live_all = homolog_present.astype(jnp.float32)
    sequence_live = lax.dynamic_slice_in_dim(
        seq_live_all, row_index * sequence_count, sequence_count, 0
    )
    live_count = jnp.sum(seq_live_all)
    residue_present = token_live_mask.astype(jnp.float32)
    row_live = lax.dynamic_slice_in_dim(residue_present, row_index * row_tokens, row_tokens, 0)
    col_live = lax.dynamic_slice_in_dim(
        residue_present, col_index * column_tokens, column_tokens, 0
    )
    left_proj = jnp.dot(
        homolog_standardized,
        product_projection[:, :outer_channel_width],
        preferred_element_type=jnp.float32,
    ).reshape(sequence_count, token_count, outer_channel_width)
    left_factor = (
        (left_proj * sequence_live[:, None, None])
        .astype(jnp.bfloat16)
        .reshape(sequence_count, token_count * outer_channel_width)
    )
    right_factor = (
        jnp.dot(
            local_norm,
            product_projection[:, outer_channel_width:],
            preferred_element_type=jnp.float32,
        )
        .astype(jnp.bfloat16)
        .reshape(sequence_count, column_tokens * outer_channel_width)
    )
    left_all = lax.all_to_all(left_factor, "row", split_axis=1, concat_axis=0, tiled=True)
    right_all = gathered_copies(right_factor, "row", 0)
    total_seqs = left_all.shape[0]
    left_all = left_all.reshape(total_seqs, row_tokens, outer_channel_width)
    right_all = right_all.reshape(total_seqs, column_tokens, outer_channel_width)
    outer_sum = jnp.einsum("sic,sjd->ijcd", left_all, right_all, preferred_element_type=jnp.float32)
    pair_live = row_live[:, None] * col_live[None, :]
    mean_scale = pair_live / jnp.maximum(pair_live * live_count, 1.0)
    pair_mean = (
        (outer_sum * mean_scale[:, :, None, None])
        .astype(jnp.bfloat16)
        .reshape(row_tokens * column_tokens, outer_channel_width * outer_channel_width)
    )
    pair_flat = pair_state.reshape(row_tokens * column_tokens, pair_width)
    pair_mid = (
        pair_flat.astype(jnp.float32)
        + jnp.dot(pair_mean, mean_matrix, preferred_element_type=jnp.float32)
    ).astype(jnp.bfloat16)
    pair_norm = normalized_rows(pair_mid)
    scores = jnp.dot(
        pair_norm, score_matrix, precision=lax.Precision.HIGHEST, preferred_element_type=jnp.float32
    )
    head_scores = jnp.transpose(scores.reshape(row_tokens, column_tokens, head_count), (2, 0, 1))
    value_columns = lax.dynamic_slice_in_dim(
        payload_projection, col_index * piece_width, piece_width, 1
    )
    gate_columns = lax.dynamic_slice_in_dim(
        switch_projection, col_index * piece_width, piece_width, 1
    )
    output_rows = lax.dynamic_slice_in_dim(
        return_projection, col_index * piece_width, piece_width, 0
    )
    payload_entries = jnp.dot(
        homolog_standardized, value_columns, preferred_element_type=jnp.float32
    ).reshape(sequence_count, token_count, piece_width)
    payload_entries = (
        (payload_entries * residue_present[None, :, None])
        .astype(jnp.bfloat16)
        .reshape(sequence_count, token_count, head_slots, slot_width)
    )
    switch_logistic = jax.nn.sigmoid(
        jnp.dot(homolog_standardized, gate_columns, preferred_element_type=jnp.float32)
    ).reshape(sequence_count, token_count, piece_width)
    spread_scores = jnp.repeat(head_scores, repeats, axis=0)
    score_rows = lax.all_to_all(spread_scores, COL, split_axis=0, concat_axis=2, tiled=True)
    blend_coefficients = softmax_last(score_rows)
    blended_result = jnp.einsum(
        "hij,sjhc->sihc",
        gathered_copies(blend_coefficients, "row", 1),
        payload_entries,
        preferred_element_type=jnp.float32,
    )
    switched_blend = (
        switch_logistic * blended_result.reshape(sequence_count, token_count, piece_width)
    ).astype(jnp.bfloat16)
    partial_sum = jnp.dot(
        switched_blend.reshape(sequence_count * token_count, piece_width),
        output_rows,
        preferred_element_type=jnp.float32,
    ).reshape(sequence_count, token_count, alignment_width)
    summed_outer = sent_and_summed(partial_sum.astype(jnp.bfloat16), COL, 1)
    hidden_pre = jnp.dot(
        pair_norm.astype(jnp.bfloat16), transition_input, preferred_element_type=jnp.float32
    )
    hidden = (jax.nn.silu(hidden_pre[:, :ff_width]) * hidden_pre[:, ff_width:]).astype(jnp.bfloat16)
    pair_new = (
        pair_mid.astype(jnp.float32)
        + jnp.dot(hidden, transition_output, preferred_element_type=jnp.float32)
    ).astype(jnp.bfloat16)
    pair_output = pair_new.reshape(row_tokens, column_tokens, pair_width)
    alignment_output = (homolog_representation.astype(jnp.float32) + summed_outer).astype(
        jnp.bfloat16
    )
    return (alignment_output, pair_output)


def solution(mesh):
    split = Mesh(mesh.devices.reshape(mesh.shape["row"], 8, 2), ("row", "col_0", "col_1"))
    placed = (
        P("row", COL, None),
        P("row", COL, None),
        P(),
        P(),
        P(),
        P(),
        P(),
        P(),
        P(),
        P(),
        P(),
        P(),
    )
    return jax.shard_map(
        body,
        mesh=split,
        in_specs=placed,
        out_specs=(P("row", COL, None), P("row", COL, None)),
        check_vma=False,
    )
```

profile of v0, /device:TPU:1, one launch (start us, length us, event | category | flops | bytes accessed | tf_op | source)
XLA Modules:
  0.0 174.0 jit_solution(14045482265264957470)
XLA Ops:
  0.7 0.7 convert_element_type.81
  1.4 8.8 %all_gather.6 = bf16[8,64,64]{2,1,0:T(8,128)(2,1)S(1)} all-gather(bf16[8,32,64]{2,1,0:T(8,128)(2,1)} %param.12), channel_id=1, replica_groups=mesh['row'=32,'col_0'=8,'col_1'=2] {'col_1'}, dimensions={1}, use_global_device_ids=true | all-gather | bytes 98304 | tf_op jit(solution)/shard_map/all_gather | solution.py:16
  10.2 22.7 %all_gather.7 = bf16[8,512,64]{2,1,0:T(8,128)(2,1)S(1)} all-gather(bf16[8,64,64]{2,1,0:T(8,128)(2,1)S(1)} %all_gather.6), channel_id=1, replica_groups=mesh['row'=32,'col_0'=8,'col_1'=2] {'col_0'}, dimensions={1}, use_global_device_ids=true | all-gather | bytes 589824 | tf_op jit(solution)/shard_map/all_gather | solution.py:16
  32.9 0.4 convert_reduce_fusion
  33.3 1.3 fusion.8
  34.6 1.2 fusion.9
  36.0 0.5 fusion.11
  36.4 0.5 copy.69
  37.0 1.0 all_to_all.35
  38.0 0.8 copy.70
  38.8 9.7 %all-to-all-start.1 = ((bf16[8,32,512]{2,0,1:T(8,128)(2,1)}), bf16[8,32,512]{2,0,1:T(8,128)(2,1)S(1)}, u32[]{:S(2)}, u32[]{:S(2)}) async-start(bf16[8,32,512]{2,0,1:T(8,128)(2,1)} %copy.70), calls=%async_computation.1 | async-start | bytes 524288 | tf_op jit(solution)/shard_map/all_to_all | solution.py:129
  48.6 0.2 fusion.24
  49.0 0.2 convolution_convert_fusion.1
  49.2 0.1 copy.66
  49.5 9.4 %all-to-all-done.1 = bf16[8,32,512]{2,0,1:T(8,128)(2,1)S(1)} async-done(((bf16[8,32,512]{2,0,1:T(8,128)(2,1)}), bf16[8,32,512]{2,0,1:T(8,128)(2,1)S(1)}, u32[]{:S(2)}, u32[]{:S(2)}) %all-to-all-start.1) | async-done | bytes 262176 | tf_op jit(solution)/shard_map/all_to_all | solution.py:129
  58.9 0.9 broadcast_in_dim.6
  59.8 4.8 %all-to-all-start = ((bf16[32,8,1024]{2,1,0:T(8,128)(2,1)}), bf16[32,8,1024]{2,1,0:T(8,128)(2,1)}, u32[]{:S(2)}, u32[]{:S(2)}) async-start(bf16[32,8,1024]{2,1,0:T(8,128)(2,1)} %broadcast_in_dim.6), calls=%async_computation | async-start | bytes 1048576 | tf_op jit(solution)/shard_map/all_to_all | solution.py:22
  64.7 0.6 convert_reduce_fusion.3
  65.3 0.7 multiply_divide_fusion
  66.1 0.6 reshape.169
  66.7 1.5 copy.72
  68.3 9.0 %all-to-all-done = bf16[32,8,1024]{2,1,0:T(8,128)(2,1)} async-done(((bf16[32,8,1024]{2,1,0:T(8,128)(2,1)}), bf16[32,8,1024]{2,1,0:T(8,128)(2,1)}, u32[]{:S(2)}, u32[]{:S(2)}) %all-to-all-start) | async-done | bytes 524320 | tf_op jit(solution)/shard_map/all_to_all | solution.py:22
  77.3 2.8 %reshape_reshape.3 = bf16[256,32,32]{2,1,0:T(8,128)(2,1)S(1)} reshape(bf16[32,8,1024]{2,1,0:T(8,128)(2,1)} %all-to-all-done) | data formatting | bytes 1048576 | tf_op jit(solution)/shard_map/reshape;reshape | solution.py:133
  80.2 9.2 %fusion = bf16[16,32,32,32]{2,3,0,1:T(8,128)(2,1)} fusion(f32[16,32]{0,1:T(8,128)S(1)} %copy.73, bf16[256,32,32,1]{2,1,0,3:T(8,128)(2,1)S(1)} %bitcast.76, bf16[256,16,32]{0,2,1:T(8,128)(2,1)} %copy.72), kind=kOutput, calls=%fused_computation.1 | convolution fusion | flops 269484032 | bytes 1837056 | tf_op jit(solution)/shard_map/sic,sjd->ijcd/dot_general | solution.py:134
  89.3 6.4 %copy.74 = bf16[16,32,32,32]{3,2,1,0:T(8,128)(2,1)} copy(bf16[16,32,32,32]{2,3,0,1:T(8,128)(2,1)} %fusion) | data formatting | bytes 2097152 | tf_op jit(solution)/shard_map/convert_element_type | solution.py:139
  95.7 6.2 %reshape.170 = bf16[512,1024]{1,0:T(8,128)(2,1)S(1)} reshape(bf16[16,32,32,32]{3,2,1,0:T(8,128)(2,1)} %copy.74) | data formatting | bytes 2097152 | tf_op jit(solution)/shard_map/reshape | solution.py:140
  101.9 0.5 fusion.51
  102.5 0.2 multiply_reduce_fusion
  102.7 0.5 fusion.19
  103.4 18.8 %all_to_all.49 = f32[16,1,512]{2,1,0:T(1,128)S(1)} all-to-all(f32[16,1,512]{2,1,0:T(1,128)S(1)} %reshape.184), channel_id=1, replica_groups=mesh['row'=32,'col_0'=8,'col_1'=2] {'col_0','col_1'}, dimensions={0} | all-to-all | bytes 65536 | tf_op jit(solution)/shard_map/all_to_all | solution.py:173
  122.3 0.5 broadcast.119
  122.8 0.7 reduce.6
  123.7 0.2 exponential_reduce_fusion
  124.2 0.8 broadcast_in_dim.8
  125.0 4.1 %all-to-all-start.3 = ((bf16[32,1,16,512]{3,2,1,0:T(8,128)(2,1)}), bf16[32,1,16,512]{3,2,1,0:T(8,128)(2,1)S(1)}, u32[]{:S(2)}, u32[]{:S(2)}) async-start(bf16[32,1,16,512]{3,2,1,0:T(8,128)(2,1)} %broadcast_in_dim.8), calls=%async_computation.3 | async-start | bytes 1048576 | tf_op jit(solution)/shard_map/all_to_all | solution.py:22
  129.2 16.6 %all-to-all-done.3 = bf16[32,1,16,512]{3,2,1,0:T(8,128)(2,1)S(1)} async-done(((bf16[32,1,16,512]{3,2,1,0:T(8,128)(2,1)}), bf16[32,1,16,512]{3,2,1,0:T(8,128)(2,1)S(1)}, u32[]{:S(2)}, u32[]{:S(2)}) %all-to-all-start.3) | async-done | bytes 524320 | tf_op jit(solution)/shard_map/all_to_all | solution.py:22
  145.8 0.7 fusion.52
  146.5 0.5 fusion.5
  147.0 0.3 convolution_convert_fusion
  147.4 0.5 copy.79
  148.0 1.5 reshape.186
  149.5 5.7 %all-to-all-start.4 = ((bf16[16,2,8192]{2,1,0:T(2,128)(2,1)}), bf16[16,2,8192]{2,1,0:T(2,128)(2,1)S(1)}, u32[]{:S(2)}, u32[]{:S(2)}) async-start(bf16[16,2,8192]{2,1,0:T(2,128)(2,1)} %reshape.186), calls=%async_computation.4 | async-start | bytes 1048576 | tf_op jit(solution)/shard_map/all_to_all | solution.py:44
  155.2 0.5 fusion.27
  155.7 1.1 fusion.12
  156.8 15.8 %all-to-all-done.4 = bf16[16,2,8192]{2,1,0:T(2,128)(2,1)S(1)} async-done(((bf16[16,2,8192]{2,1,0:T(2,128)(2,1)}), bf16[16,2,8192]{2,1,0:T(2,128)(2,1)S(1)}, u32[]{:S(2)}, u32[]{:S(2)}) %all-to-all-start.4) | async-done | bytes 524320 | tf_op jit(solution)/shard_map/all_to_all | solution.py:44
  172.5 0.7 reshape.187
  173.2 0.2 convert_reduce_fusion.1
  173.4 0.6 fusion.26
  (48 shorter events, 1.6 us)
Async XLA Ops:
  0.6 154.5 %copy-start = (bf16[128,1024]{1,0:T(8,128)(2,1)S(1)}, bf16[128,1024]{1,0:T(8,128)(2,1)}, u32[]{:S(2)}) copy-start(bf16[128,1024]{1,0:T(8,128)(2,1)} %param.22) | copy-start | bytes 786436
  32.9 3.0 %copy-start.4 = (bf16[64,64]{1,0:T(8,128)(2,1)S(1)}, bf16[64,64]{1,0:T(8,128)(2,1)}, u32[]{:S(2)}) copy-start(bf16[64,64]{1,0:T(8,128)(2,1)} %param.16) | copy-start | bytes 24580
  36.4 12.1 %copy-start.1 = (bf16[8,32,64]{2,1,0:T(8,128)(2,1)S(1)}, bf16[8,32,64]{2,1,0:T(8,128)(2,1)}, u32[]{:S(2)}) copy-start(bf16[8,32,64]{2,1,0:T(8,128)(2,1)} %param.12) | copy-start | bytes 98308
  36.9 27.6 %copy-start.8 = (s32[512]{0:T(512)S(1)}, s32[512]{0:T(512)}, u32[]{:S(2)}) copy-start(s32[512]{0:T(512)} %param.15) | copy-start | bytes 6148
  36.9 27.8 %copy-start.9 = (s32[256]{0:T(256)S(1)}, s32[256]{0:T(256)}, u32[]{:S(2)}) copy-start(s32[256]{0:T(256)} %param.14) | copy-start | bytes 3076
  38.8 20.1 %all-to-all-start.1 = ((bf16[8,32,512]{2,0,1:T(8,128)(2,1)}), bf16[8,32,512]{2,0,1:T(8,128)(2,1)S(1)}, u32[]{:S(2)}, u32[]{:S(2)}) async-start(bf16[8,32,512]{2,0,1:T(8,128)(2,1)} %copy.70), calls=%async_computation.1 | async-start | bytes 524288 | tf_op jit(solution)/shard_map/all_to_all | solution.py:129
  59.8 17.5 %all-to-all-start = ((bf16[32,8,1024]{2,1,0:T(8,128)(2,1)}), bf16[32,8,1024]{2,1,0:T(8,128)(2,1)}, u32[]{:S(2)}, u32[]{:S(2)}) async-start(bf16[32,8,1024]{2,1,0:T(8,128)(2,1)} %broadcast_in_dim.6), calls=%async_computation | async-start | bytes 1048576 | tf_op jit(solution)/shard_map/all_to_all | solution.py:22
  95.7 6.2 %copy-start.2 = (bf16[1024,128]{1,0:T(8,128)(2,1)S(1)}, bf16[1024,128]{1,0:T(8,128)(2,1)}, u32[]{:S(2)}) copy-start(bf16[1024,128]{1,0:T(8,128)(2,1)} %param.17) | copy-start | bytes 786436
  95.7 6.2 %copy-start.3 = (bf16[16,32,128]{2,1,0:T(8,128)(2,1)S(1)}, bf16[16,32,128]{2,1,0:T(8,128)(2,1)}, u32[]{:S(2)}) copy-start(bf16[16,32,128]{2,1,0:T(8,128)(2,1)} %param.13) | copy-start | bytes 393220
  95.7 7.0 %copy-start.7 = (f32[128,8]{0,1:T(8,128)S(1)}, f32[128,8]{0,1:T(8,128)}, u32[]{:S(2)}) copy-start(f32[128,8]{0,1:T(8,128)} %param.18) | copy-start | bytes 12292
  102.4 43.3 %copy-start.5 = (bf16[64,256]{1,0:T(8,128)(2,1)S(1)}, bf16[64,256]{1,0:T(8,128)(2,1)}, u32[]{:S(2)}) copy-start(bf16[64,256]{1,0:T(8,128)(2,1)} %param.19) | copy-start | bytes 98308
  124.0 22.5 %copy-start.11 = (bf16[64,256]{1,0:T(8,128)(2,1)S(1)}, bf16[64,256]{1,0:T(8,128)(2,1)}, u32[]{:S(2)}) copy-start(bf16[64,256]{1,0:T(8,128)(2,1)} %param.20) | copy-start | bytes 98308
  125.0 20.7 %all-to-all-start.3 = ((bf16[32,1,16,512]{3,2,1,0:T(8,128)(2,1)}), bf16[32,1,16,512]{3,2,1,0:T(8,128)(2,1)S(1)}, u32[]{:S(2)}, u32[]{:S(2)}) async-start(bf16[32,1,16,512]{3,2,1,0:T(8,128)(2,1)} %broadcast_in_dim.8), calls=%async_computation.3 | async-start | bytes 1048576 | tf_op jit(solution)/shard_map/all_to_all | solution.py:22
  129.2 17.8 %copy-start.6 = (bf16[256,64]{0,1:T(8,128)(2,1)S(1)}, bf16[256,64]{0,1:T(8,128)(2,1)}, u32[]{:S(2)}) copy-start(bf16[256,64]{0,1:T(8,128)(2,1)} %param.21) | copy-start | bytes 98308
  149.5 6.2 %copy-start.10 = (bf16[512,128]{1,0:T(8,128)(2,1)S(1)}, bf16[512,128]{1,0:T(8,128)(2,1)}, u32[]{:S(2)}) copy-start(bf16[512,128]{1,0:T(8,128)(2,1)} %param.23) | copy-start | bytes 393220
  149.5 23.0 %all-to-all-start.4 = ((bf16[16,2,8192]{2,1,0:T(2,128)(2,1)}), bf16[16,2,8192]{2,1,0:T(2,128)(2,1)S(1)}, u32[]{:S(2)}, u32[]{:S(2)}) async-start(bf16[16,2,8192]{2,1,0:T(2,128)(2,1)} %reshape.186), calls=%async_computation.4 | async-start | bytes 1048576 | tf_op jit(solution)/shard_map/all_to_all | solution.py:44
where the time goes:
time: 175 us; the launch traced here: 174 us
  waiting for transfers between devices  50.7 us (29%)
  blocking collectives  50.4 us (29%)
  local copies, waits for them, and re-layouts  26 us (15%)
  starting transfers between devices  24.3 us (14%)
  matrix products  14 us (8%)
  other arithmetic  7.64 us (4%)
    all_gather x2, blocking collectives, gather_axes(): whole = lax.all_gather(whole, axes[number], axis=dim, tiled=True)  31.6 us
    all_to_all x2, waiting for transfers between devices, from_everyone(): return lax.all_to_all(copies, axis, split_axis=0, concat_axis=0, tiled=True)  25.6 us
    all_to_all x1, blocking collectives, body(): lax.all_to_all(spread_scores, COL, split_axis=0, concat_axis=2, tiled=True)  18.8 us
    all_to_all x1, waiting for transfers between devices, sent_and_summed(): lax.all_to_all(pieces, axis, split_axis=0, concat_axis=0, tiled=True)  15.8 us
    all_to_all x1, starting transfers between devices, body(): lax.all_to_all(left_factor, 'row', split_axis=1, concat_axis=0, tiled=True)  9.67 us
    all_to_all x1, waiting for transfers between devices, body(): lax.all_to_all(left_factor, 'row', split_axis=1, concat_axis=0, tiled=True)  9.41 us
    dot_general x1, matrix products, body(): jnp.einsum('sic,sjd->ijcd', left_all, right_all, preferred_element_type=j...  9.16 us
    all_to_all x2, starting transfers between devices, from_everyone(): return lax.all_to_all(copies, axis, split_axis=0, concat_axis=0, tiled=True)  8.94 us
  transfers between devices with their start and end apart: 4, of which 4 were waited for; matrix products, arithmetic and copies ran while one was open for 4% of the time, Pallas kernels for 0%

commit v1 on v0

v1 whole, which is shorter than its diff:
```python
import functools

import jax
import jax.numpy as jnp
from jax import lax
from jax.experimental import pallas as pl
from jax.experimental.pallas import tpu as pltpu
from jax.sharding import Mesh
from jax.sharding import PartitionSpec as P

F32 = jnp.float32
BF16 = jnp.bfloat16
MESH = pl.DeviceIdType.MESH
epsilon = 1e-05

X, K = 4, 2
SEQ = 8
TOK = 32
ROW = 16
HEADS = 8


def iota(shape, dim):
    return lax.broadcasted_iota(jnp.int32, shape, dim)


def one_hot(condition):
    return jnp.where(condition, 1.0, 0.0).astype(BF16)


def dot(a, b):
    return jnp.dot(a, b, preferred_element_type=F32)


def dot_nt(a, b, precision=None):
    return lax.dot_general(
        a, b, (((1,), (1,)), ((), ())), precision=precision, preferred_element_type=F32
    )


def normalized(source):
    center = source - jnp.mean(source, axis=-1, keepdims=True)
    spread = jnp.mean(center * center, axis=-1, keepdims=True)
    return center * lax.rsqrt(spread + epsilon)


def kernel(
    Y,
    Z,
    h_ref,
    pair_ref,
    seq_ref,
    tok_ref,
    pp_ref,
    mm_ref,
    smt_ref,
    pay_ref,
    sw_ref,
    rett_ref,
    ti_ref,
    to_ref,
    align_ref,
    pout_ref,
    RB,
    LS,
    LX,
    LZ,
    LB,
    HB,
    EY,
    EZ,
    EX,
    MF,
    WB,
    AB,
    VB,
    NB,
    MID,
    PNB,
    ry_s,
    rx_s,
    r_r,
    lx_s,
    lx_r,
    lz_s,
    lz_r,
    ly_s,
    ly_r,
    lk_s,
    hz_s,
    hk_s,
    h_r,
    ey_s,
    ey_r,
    ez_s,
    ez_r,
    ex_s,
    ex_r,
):
    R = Y * X
    C = Z * K
    NS = R * SEQ
    NT = C * TOK
    y, x = lax.axis_index("y"), lax.axis_index("x")
    z, k = lax.axis_index("z"), lax.axis_index("k")
    row = y * X + x
    col = z * K + k
    owner = k == x // 2

    def remote(src, dst, send, recv, **to):
        return pltpu.make_async_remote_copy(
            src_ref=src,
            dst_ref=dst,
            send_sem=send,
            recv_sem=recv,
            device_id=to,
            device_id_type=MESH,
        )

    barrier = pltpu.get_barrier_semaphore()
    for t in range(1, X):
        pl.semaphore_signal(
            barrier, inc=1, device_id={"x": lax.rem(x + t, X)}, device_id_type=MESH
        )
    for t in range(1, Y):
        pl.semaphore_signal(
            barrier, inc=1, device_id={"y": lax.rem(y + t, Y)}, device_id_type=MESH
        )
    for t in range(1, C):
        other = lax.rem(col + t, C)
        pl.semaphore_signal(
            barrier,
            inc=1,
            device_id={"z": other // K, "k": lax.rem(other, K)},
            device_id_type=MESH,
        )

    hf = h_ref[...].reshape(SEQ * TOK, 64).astype(F32)
    norm_f = normalized(hf)
    NB[...] = norm_f.astype(BF16)
    tokens = tok_ref[...].astype(F32)
    seqs = seq_ref[...].astype(F32)
    hit = iota((TOK, NT), 1) == col * TOK + iota((TOK, NT), 0)
    live_tok = jnp.sum(jnp.where(hit, tokens, 0.0), axis=1, keepdims=True)
    live_tok = jnp.concatenate([live_tok] * SEQ, axis=0)
    hit = iota((SEQ * TOK, NS), 1) == row * SEQ + iota((SEQ * TOK, NS), 0) // TOK
    live_seq = jnp.sum(jnp.where(hit, seqs, 0.0), axis=1, keepdims=True)
    inverse_count = 1.0 / jnp.maximum(jnp.sum(seqs, axis=1, keepdims=True), 1.0)
    norm = (norm_f * live_tok).astype(BF16)

    pp = pp_ref[...]
    right_t = dot_nt(one_hot(iota((32, 64), 1) == 32 + iota((32, 64), 0)), pp).astype(BF16)
    spread = []
    for s in range(SEQ):
        one = norm[s * TOK : (s + 1) * TOK]
        spread.append(dot_nt(right_t, jnp.concatenate([one] * 4, axis=0)))
    spread = jnp.concatenate(spread, axis=0)
    mine = iota((256, 128), 0) % 4 == iota((256, 128), 1) // 32
    spread = jnp.where(mine, spread, 0.0).astype(BF16)
    a, b = iota((64, 256), 0), iota((64, 256), 1)
    pick = one_hot((a % 8 == b // 32) & ((b % 32) // 4 == ((a // 8) % 2) * 4 + a // 16))
    packed = dot(pick, spread).astype(BF16)
    for t in range(4):
        RB[row, :, t * 128 : (t + 1) * 128] = packed[t * 16 : (t + 1) * 16]

    left_w = dot(pp, one_hot(iota((64, 128), 0) == iota((64, 128), 1) % 32)).astype(BF16)
    spread = dot(norm, left_w) * live_seq
    spread = jnp.where(mine, spread, 0.0).astype(BF16)
    pick = one_hot(
        (a % 8 == b // 32) & ((b % 32) // 4 == 4 * (a // 32) + 2 * ((a // 8) % 2) + (a // 16) % 2)
    )
    packed = dot(pick, spread).astype(BF16)
    for h in range(2):
        for t in range(2):
            LS[h, :, t * 128 : (t + 1) * 128] = packed[(h * 2 + t) * 16 : (h * 2 + t + 1) * 16]

    u, v = iota((64, 128), 0), iota((64, 128), 1)
    HB[col] = (
        dot(norm[:128], one_hot(u == v)) + dot(norm[128:], one_hot(u + 64 == v))
    ).astype(BF16)

    pl.semaphore_wait(barrier, (X - 1) + (Y - 1) + (C - 1))

    for h in range(2):
        to = 2 * k + h

        @pl.when(to != x)
        def _():
            remote(LS.at[h], LX.at[x], lx_s.at[h], lx_r.at[x], x=to).start()

        @pl.when(to == x)
        def _():
            LX[x] = LS[h]

    def right_y(t):
        return remote(
            RB.at[row], RB.at[row], ry_s.at[t], r_r.at[row], y=lax.rem(y + t, Y)
        )

    def right_x(block, t):
        r = block * X + x
        return remote(
            RB.at[r], RB.at[r], rx_s.at[block, t], r_r.at[r], x=lax.rem(x + t, X)
        )

    def right_arrived(r):
        remote(RB.at[r], RB.at[r], ry_s.at[0], r_r.at[r], x=x).wait_recv()

    for t in range(1, Y):
        right_y(t).start()
    for t in range(1, X):
        right_x(y, t).start()

    MF[...] = mm_ref[...].astype(F32)
    WB[...] = jnp.zeros_like(WB)

    def left_z(t):
        return remote(LZ.at[z], LZ.at[z], lz_s.at[t], lz_r.at[z], z=lax.rem(z + t, Z))

    def hz(t):
        return remote(HB.at[col], HB.at[col], hz_s.at[t], h_r.at[col], z=lax.rem(z + t, Z))

    @pl.when(owner)
    def _():
        for t in range(1, X):
            other = lax.rem(x + t, X)
            remote(LX.at[other], LX.at[other], lx_s.at[0], lx_r.at[other], x=x).wait_recv()
        LZ[z] = LX[...]
        for t in range(1, Z):
            left_z(t).start()

    for t in range(1, Z):
        hz(t).start()

    for d in range(32):
        part = MF[pl.ds(d, 32, stride=32), :].astype(BF16)
        for i in range(4):
            WB[d * 128 + i * 32 : d * 128 + (i + 1) * 32, i * 128 : (i + 1) * 128] = part

    def left_y(block):
        return remote(LZ.at[block], LB.at[y], ly_s.at[block], ly_r.at[y], y=block)

    def left_k(block):
        return remote(LB.at[block], LB.at[block], lk_s.at[block], ly_r.at[block], k=1 - k)

    for t in range(Y):
        if t > 0:
            block = lax.rem(y + Y - t, Y)
            right_arrived(block * X + x)
            for u_ in range(1, X):
                right_x(block, u_).start()
        at = lax.rem(z + Z - t, Z)

        @pl.when(owner)
        def _():
            if t > 0:
                remote(LZ.at[at], LZ.at[at], lz_s.at[0], lz_r.at[at], z=z).wait_recv()

            @pl.when(at != y)
            def _():
                left_y(at).start()

            @pl.when(at == y)
            def _():
                LB[y] = LZ[y]

    @pl.when(owner)
    def _():
        left_k(y).start()
        for t in range(1, Y):
            block = lax.rem(y + Y - t, Y)
            remote(LZ.at[0], LB.at[block], ly_s.at[0], ly_r.at[block], y=y).wait_recv()
            left_k(block).start()

    def hk(block):
        c = block * K + k
        return remote(HB.at[c], HB.at[c], hk_s.at[block], h_r.at[c], k=1 - k)

    def h_arrived(c):
        remote(HB.at[c], HB.at[c], hz_s.at[0], h_r.at[c], z=z).wait_recv()

    hk(z).start()
    for t in range(1, Z):
        block = lax.rem(z + Z - t, Z)
        h_arrived(block * K + k)
        hk(block).start()

    for t in range(1, X):
        other = lax.rem(x + t, X)
        for block in range(Y):
            right_arrived(block * X + other)

    @pl.when(jnp.logical_not(owner))
    def _():
        for block in range(Y):
            remote(LZ.at[0], LB.at[block], ly_s.at[0], ly_r.at[block], y=y).wait_recv()

    left = LB[...].astype(F32).reshape(R, 2, SEQ, 256)
    left = jnp.concatenate(
        [left[:, 0].reshape(NS, 256), left[:, 1].reshape(NS, 256)], axis=1
    ).astype(BF16)
    for half in range(2):
        right = RB[...].astype(F32).reshape(R, 2, SEQ, 512)[:, half].reshape(NS, 512)
        right = jnp.transpose(right).astype(BF16)
        for part in range(2):
            outer = dot(right[part * 256 : (part + 1) * 256], left).astype(BF16)
            for dd in range(8):
                d = half * 16 + part * 8 + dd
                for g in range(4):
                    AB[g * 32 : (g + 1) * 32, d * 128 : (d + 1) * 128] = outer[
                        dd * 32 : (dd + 1) * 32, g * 128 : (g + 1) * 128
                    ]
    mean = dot(AB[...], WB[...]) * inverse_count
    mean = jnp.concatenate(
        [
            mean[(i // 4) * 32 : (i // 4 + 1) * 32, (i % 4) * 128 : (i % 4 + 1) * 128]
            for i in range(ROW)
        ],
        axis=0,
    )
    pair_mid = (pair_ref[...].reshape(ROW * TOK, 128).astype(F32) + mean).astype(BF16)
    MID[...] = pair_mid
    pair_norm = normalized(pair_mid.astype(F32))
    PNB[...] = pair_norm.astype(BF16)
    score_w = jnp.concatenate(
        [jnp.broadcast_to(smt_ref[h : h + 1, :], (ROW, 128)) for h in range(HEADS)], axis=0
    )
    every = dot_nt(pair_norm, score_w, lax.Precision.HIGHEST)
    lane_i = iota((TOK, 128), 1) % ROW
    scores = jnp.zeros((TOK, 128), F32)
    for i in range(ROW):
        scores = jnp.where(lane_i == i, every[i * TOK : (i + 1) * TOK], scores)
    shift = jnp.max(scores, axis=0, keepdims=True).astype(BF16).astype(F32)
    EY[y, 0:TOK, :] = jnp.exp(scores - shift).astype(BF16)
    EY[y, TOK : TOK + 16, :] = jnp.broadcast_to(shift, (16, 128)).astype(BF16)

    def ey(t):
        return remote(EY.at[y], EY.at[y], ey_s.at[t], ey_r.at[y], y=lax.rem(y + t, Y))

    def ez(block):
        return remote(
            EY.at[block], EZ.at[col], ez_s.at[block], ez_r.at[col], z=block, k=x // 2
        )

    def ex(t):
        return remote(
            EX.at[x % 2], EX.at[x % 2], ex_s.at[t], ex_r.at[x % 2], x=lax.rem(x + t, X)
        )

    def forward_z(block):
        away = jnp.logical_or(block != z, jnp.logical_not(owner))

        @pl.when(away)
        def _():
            ez(block).start()

        @pl.when(jnp.logical_not(away))
        def _():
            EZ[col] = EY[z]

    def transition(part):
        rows = slice(part * 128, (part + 1) * 128)
        pre = dot(PNB[rows, :], ti_ref[...])
        gate = pre[:, :512]
        hidden = (gate / (1.0 + jnp.exp(-gate)) * pre[:, 512:]).astype(BF16)
        out = (MID[rows, :].astype(F32) + dot(hidden, to_ref[...])).astype(BF16)
        pout_ref[part * 4 : (part + 1) * 4] = out.reshape(4, TOK, 128)

    for t in range(1, Y):
        ey(t).start()
    forward_z(y)
    transition(0)
    for t in range(1, Y):
        block = lax.rem(y + Y - t, Y)
        remote(EY.at[block], EY.at[block], ey_s.at[0], ey_r.at[block], y=y).wait_recv()
        forward_z(block)
    transition(1)
    transition(2)

    @pl.when(owner)
    def _():
        for t in range(1, C):
            c = lax.rem(col + t, C)
            remote(EY.at[0], EZ.at[c], ez_s.at[0], ez_r.at[c], z=z).wait_recv()
        shifts = EZ[:, TOK : TOK + 16, :].astype(F32)[:, 0:1, :]
        factor = jnp.exp(shifts - jnp.max(shifts, axis=0, keepdims=True))
        weights = EZ[:, 0:TOK, :].astype(F32) * factor
        total = jnp.sum(jnp.sum(weights, axis=0, keepdims=True), axis=1, keepdims=True)
        EX[x % 2] = (weights / total).astype(BF16).reshape(NT, 128)
        for t in range(1, X):
            ex(t).start()

    transition(3)

    for t in range(Z):
        h_arrived(t * K + 1 - k)
    zeros = jnp.zeros((64, 256), BF16)
    for side in range(2):
        pay = jnp.concatenate(
            [pay_ref[...], zeros] if side == 0 else [zeros, pay_ref[...]], axis=0
        )
        for s in range(4):
            rows = HB[:, s * TOK : (s + 1) * TOK, :].reshape(NT, 128)
            VB[side * 4 + s] = dot(rows, pay).astype(BF16)
    gate = jax.nn.sigmoid(dot(NB[...], sw_ref[...]))

    for h in range(2):

        @pl.when(x != 2 * k + h)
        def _():
            remote(EX.at[h], EX.at[h], ex_s.at[0], ex_r.at[h], x=x).wait_recv()

    weights = jnp.concatenate(
        [jnp.transpose(EX[h].astype(F32)).astype(BF16) for h in range(2)], axis=0
    )
    head = iota((ROW, 256), 1) // 32
    averages = []
    for s in range(SEQ):
        full = dot(weights, VB[s])
        for half in range(2):
            average = jnp.zeros((ROW, 256), F32)
            for g in range(HEADS):
                start = half * 128 + g * ROW
                average = jnp.where(head == g, full[start : start + ROW], average)
            averages.append(average)
    gated = (gate * jnp.concatenate(averages, axis=0)).astype(BF16)
    out = h_ref[...].reshape(SEQ * TOK, 64).astype(F32) + dot_nt(gated, rett_ref[...])
    align_ref[...] = out.astype(BF16).reshape(SEQ, TOK, 64)

    for h in range(2):

        @pl.when(2 * k + h != x)
        def _():
            remote(LS.at[h], LX.at[x], lx_s.at[h], lx_r.at[x], x=2 * k + h).wait_send()

    for t in range(1, Y):
        right_y(t).wait_send()
        ey(t).wait_send()
    for block in range(Y):
        for t in range(1, X):
            right_x(block, t).wait_send()
    for t in range(1, Z):
        hz(t).wait_send()
    for block in range(Z):
        hk(block).wait_send()

        @pl.when(jnp.logical_or(block != z, jnp.logical_not(owner)))
        def _():
            ez(block).wait_send()

    @pl.when(owner)
    def _():
        for t in range(1, Z):
            left_z(t).wait_send()
        for block in range(Z):

            @pl.when(block != y)
            def _():
                left_y(block).wait_send()

            left_k(block).wait_send()
        for t in range(1, X):
            ex(t).wait_send()


def body(h, pair, seq, tok, pp, mm, sm, pay, sw, ret, ti, to, *, Y, Z):
    R, C = Y * X, Z * K
    NT = C * TOK
    dma = pltpu.SemaphoreType.DMA
    vmem = pl.BlockSpec(memory_space=pltpu.VMEM)
    return pl.pallas_call(
        functools.partial(kernel, Y, Z),
        out_shape=(
            jax.ShapeDtypeStruct(h.shape, BF16),
            jax.ShapeDtypeStruct(pair.shape, BF16),
        ),
        in_specs=[vmem] * 12,
        out_specs=(vmem, vmem),
        scratch_shapes=[
            pltpu.VMEM((R, 16, 512), BF16),
            pltpu.VMEM((2, 16, 256), BF16),
            pltpu.VMEM((X, 16, 256), BF16),
            pltpu.VMEM((Z, X, 16, 256), BF16),
            pltpu.VMEM((Y, X, 16, 256), BF16),
            pltpu.VMEM((C, 128, 128), BF16),
            pltpu.VMEM((Y, TOK + 16, 128), BF16),
            pltpu.VMEM((C, TOK + 16, 128), BF16),
            pltpu.VMEM((2, NT, 128), BF16),
            pltpu.VMEM((1024, 128), F32),
            pltpu.VMEM((4096, 512), BF16),
            pltpu.VMEM((128, 4096), BF16),
            pltpu.VMEM((SEQ, NT, 256), BF16),
            pltpu.VMEM((256, 64), BF16),
            pltpu.VMEM((512, 128), BF16),
            pltpu.VMEM((512, 128), BF16),
            dma((Y,)),
            dma((Y, X)),
            dma((R,)),
            dma((2,)),
            dma((X,)),
            dma((Z,)),
            dma((Z,)),
            dma((Z,)),
            dma((Y,)),
            dma((Y,)),
            dma((Z,)),
            dma((Z,)),
            dma((C,)),
            dma((Y,)),
            dma((Y,)),
            dma((Z,)),
            dma((C,)),
            dma((X,)),
            dma((2,)),
        ],
        compiler_params=pltpu.CompilerParams(
            collective_id=0, has_side_effects=True, vmem_limit_bytes=48 * 1024 * 1024
        ),
        cost_estimate=pl.CostEstimate(
            flops=3_000_000_000, bytes_accessed=2_000_000, transcendentals=400_000
        ),
    )(h, pair, seq.reshape(1, -1), tok.reshape(1, -1), pp, mm, sm.T, pay, sw, ret.T, ti, to)


def solution(mesh):
    Y, Z = mesh.shape["row"] // X, mesh.shape["col"] // K
    split = Mesh(mesh.devices.reshape(Y, X, Z, K), ("y", "x", "z", "k"))
    tiled = P(("y", "x"), ("z", "k"), None)
    return jax.shard_map(
        functools.partial(body, Y=Y, Z=Z),
        mesh=split,
        in_specs=(tiled, tiled) + (P(),) * 10,
        out_specs=(tiled, tiled),
        check_vma=False,
    )
```

time: 175 us -> 60 us (0.34)
  the two profiles are of different devices: /device:TPU:1 before, /device:TPU:64 now
where the time goes in v1:
time: 60 us; the launch traced here: 59.4 us
  Pallas kernels  49.2 us (82%)
  local copies, waits for them, and re-layouts  9.51 us (16%)
  between operations  0.68 us (1%)
    pallas_call x1, Pallas kernels, body(): pl.pallas_call(functools.partial(kernel, Y, Z), out_shape=(jax.ShapeDtype...  49.2 us
    unnamed x26, local copies, waits for them, and re-layouts  9.51 us

profile of v1, /device:TPU:64, one launch (start us, length us, event | category | flops | bytes accessed | tf_op | source)
XLA Modules:
  0.0 59.4 jit_solution(7212130434672395727)
XLA Ops:
  0.6 0.0 copy-start.9
  0.6 0.0 copy-start.10
  0.7 0.0 copy-start.11
  0.7 0.7 %copy-done.9 = f32[128,8]{0,1:T(8,128)S(1)} copy-done((f32[128,8]{0,1:T(8,128)S(1)}, f32[128,8]{0,1:T(8,128)}, u32[]{:S(2)}) %copy-start.9) | copy-done | bytes 4120
  1.3 0.0 copy-done.10
  1.3 0.0 copy-done.11
  1.3 0.0 copy-start
  1.3 0.9 %copy-done = bf16[1024,128]{1,0:T(8,128)(2,1)S(1)} copy-done((bf16[1024,128]{1,0:T(8,128)(2,1)S(1)}, bf16[1024,128]{1,0:T(8,128)(2,1)}, u32[]{:S(2)}) %copy-start) | copy-done | bytes 262168
  2.3 0.0 copy-start.1
  2.3 0.9 %copy-done.1 = bf16[128,1024]{1,0:T(8,128)(2,1)S(1)} copy-done((bf16[128,1024]{1,0:T(8,128)(2,1)S(1)}, bf16[128,1024]{1,0:T(8,128)(2,1)}, u32[]{:S(2)}) %copy-start.1) | copy-done | bytes 262168
  3.2 0.0 copy-start.2
  3.2 0.9 %copy-done.2 = bf16[16,32,128]{2,1,0:T(8,128)(2,1)S(1)} copy-done((bf16[16,32,128]{2,1,0:T(8,128)(2,1)S(1)}, bf16[16,32,128]{2,1,0:T(8,128)(2,1)}, u32[]{:S(2)}) %copy-start.2) | copy-done | bytes 131096
  4.2 0.0 copy-start.3
  4.2 0.9 %copy-done.3 = bf16[512,128]{1,0:T(8,128)(2,1)S(1)} copy-done((bf16[512,128]{1,0:T(8,128)(2,1)S(1)}, bf16[512,128]{1,0:T(8,128)(2,1)}, u32[]{:S(2)}) %copy-start.3) | copy-done | bytes 131096
  5.1 0.0 copy-start.4
  5.1 0.8 %copy-done.4 = bf16[8,32,64]{2,1,0:T(8,128)(2,1)S(1)} copy-done((bf16[8,32,64]{2,1,0:T(8,128)(2,1)S(1)}, bf16[8,32,64]{2,1,0:T(8,128)(2,1)}, u32[]{:S(2)}) %copy-start.4) | copy-done | bytes 32792
  5.9 0.0 copy-start.5
  5.9 0.8 %copy-done.5 = bf16[64,256]{1,0:T(8,128)(2,1)S(1)} copy-done((bf16[64,256]{1,0:T(8,128)(2,1)S(1)}, bf16[64,256]{1,0:T(8,128)(2,1)}, u32[]{:S(2)}) %copy-start.5) | copy-done | bytes 32792
  6.7 0.0 copy-start.6
  6.7 0.8 %copy-done.6 = bf16[64,256]{1,0:T(8,128)(2,1)S(1)} copy-done((bf16[64,256]{1,0:T(8,128)(2,1)S(1)}, bf16[64,256]{1,0:T(8,128)(2,1)}, u32[]{:S(2)}) %copy-start.6) | copy-done | bytes 32792
  7.4 0.0 copy-start.7
  7.4 0.8 %copy-done.7 = bf16[256,64]{0,1:T(8,128)(2,1)S(1)} copy-done((bf16[256,64]{0,1:T(8,128)(2,1)S(1)}, bf16[256,64]{0,1:T(8,128)(2,1)}, u32[]{:S(2)}) %copy-start.7) | copy-done | bytes 32792
  8.2 0.0 copy-start.8
  8.2 0.7 %copy-done.8 = bf16[64,64]{1,0:T(8,128)(2,1)S(1)} copy-done((bf16[64,64]{1,0:T(8,128)(2,1)S(1)}, bf16[64,64]{1,0:T(8,128)(2,1)}, u32[]{:S(2)}) %copy-start.8) | copy-done | bytes 8216
  8.9 49.2 %shard_map.131 = (bf16[8,32,64]{2,1,0:T(8,128)(2,1)S(1)}, bf16[16,32,128]{2,1,0:T(8,128)(2,1)S(1)}) custom-call(bf16[8,32,64]{2,1,0:T(8,128)(2,1)S(1)} %copy-done.4, bf16[16,32,128]{2,1,0:T(8,128)(2,1)S(1)} %copy-done.2, s32[1,256]{1,0:T(1,128)S(1)} %bitcast.7, s32[1,512]{1,0:T(1,128)S(1)} %bitcast.6, bf16[64,64]{1,0:T(8,128)(2,1)S(1)} %copy-done.8, ...), custom_call_target="tpu_custom_call" | custom-call | flops 3000000000 | bytes 2000000 | tf_op jit(solution)/shard_map/pallas_call | solution.py:471
  58.1 0.6 %copy.16 = bf16[8,32,64]{2,1,0:T(8,128)(2,1)} copy(bf16[8,32,64]{2,1,0:T(8,128)(2,1)S(1)} %get-tuple-element.4) | data formatting | bytes 65536
  58.8 0.7 %copy.17 = bf16[16,32,128]{2,1,0:T(8,128)(2,1)} copy(bf16[16,32,128]{2,1,0:T(8,128)(2,1)S(1)} %get-tuple-element.5) | data formatting | bytes 262144
Async XLA Ops:
  0.6 0.7 %copy-start.9 = (f32[128,8]{0,1:T(8,128)S(1)}, f32[128,8]{0,1:T(8,128)}, u32[]{:S(2)}) copy-start(f32[128,8]{0,1:T(8,128)} %param.18) | copy-start | bytes 12292
  0.6 0.7 %copy-start.10 = (s32[512]{0:T(512)S(1)}, s32[512]{0:T(512)}, u32[]{:S(2)}) copy-start(s32[512]{0:T(512)} %param.15) | copy-start | bytes 6148
  0.7 0.7 %copy-start.11 = (s32[256]{0:T(256)S(1)}, s32[256]{0:T(256)}, u32[]{:S(2)}) copy-start(s32[256]{0:T(256)} %param.14) | copy-start | bytes 3076
  1.3 0.9 %copy-start = (bf16[1024,128]{1,0:T(8,128)(2,1)S(1)}, bf16[1024,128]{1,0:T(8,128)(2,1)}, u32[]{:S(2)}) copy-start(bf16[1024,128]{1,0:T(8,128)(2,1)} %mm_ref.1) | copy-start | bytes 786436
  2.3 0.9 %copy-start.1 = (bf16[128,1024]{1,0:T(8,128)(2,1)S(1)}, bf16[128,1024]{1,0:T(8,128)(2,1)}, u32[]{:S(2)}) copy-start(bf16[128,1024]{1,0:T(8,128)(2,1)} %ti_ref.1) | copy-start | bytes 786436
  3.2 0.9 %copy-start.2 = (bf16[16,32,128]{2,1,0:T(8,128)(2,1)S(1)}, bf16[16,32,128]{2,1,0:T(8,128)(2,1)}, u32[]{:S(2)}) copy-start(bf16[16,32,128]{2,1,0:T(8,128)(2,1)} %pair_ref.1) | copy-start | bytes 393220
  4.2 0.9 %copy-start.3 = (bf16[512,128]{1,0:T(8,128)(2,1)S(1)}, bf16[512,128]{1,0:T(8,128)(2,1)}, u32[]{:S(2)}) copy-start(bf16[512,128]{1,0:T(8,128)(2,1)} %to_ref.1) | copy-start | bytes 393220
  5.1 0.8 %copy-start.4 = (bf16[8,32,64]{2,1,0:T(8,128)(2,1)S(1)}, bf16[8,32,64]{2,1,0:T(8,128)(2,1)}, u32[]{:S(2)}) copy-start(bf16[8,32,64]{2,1,0:T(8,128)(2,1)} %h_ref.1) | copy-start | bytes 98308
  5.9 0.8 %copy-start.5 = (bf16[64,256]{1,0:T(8,128)(2,1)S(1)}, bf16[64,256]{1,0:T(8,128)(2,1)}, u32[]{:S(2)}) copy-start(bf16[64,256]{1,0:T(8,128)(2,1)} %pay_ref.1) | copy-start | bytes 98308
  6.7 0.8 %copy-start.6 = (bf16[64,256]{1,0:T(8,128)(2,1)S(1)}, bf16[64,256]{1,0:T(8,128)(2,1)}, u32[]{:S(2)}) copy-start(bf16[64,256]{1,0:T(8,128)(2,1)} %sw_ref.1) | copy-start | bytes 98308
  7.4 0.8 %copy-start.7 = (bf16[256,64]{0,1:T(8,128)(2,1)S(1)}, bf16[256,64]{0,1:T(8,128)(2,1)}, u32[]{:S(2)}) copy-start(bf16[256,64]{0,1:T(8,128)(2,1)} %param.21) | copy-start | bytes 98308
  8.2 0.7 %copy-start.8 = (bf16[64,64]{1,0:T(8,128)(2,1)S(1)}, bf16[64,64]{1,0:T(8,128)(2,1)}, u32[]{:S(2)}) copy-start(bf16[64,64]{1,0:T(8,128)(2,1)} %pp_ref.1) | copy-start | bytes 24580

commit v2 on v1

v2 whole, which is shorter than its diff:
```python
import functools

import jax
import jax.numpy as jnp
from jax import lax
from jax.experimental import pallas as pl
from jax.experimental.pallas import tpu as pltpu
from jax.sharding import Mesh
from jax.sharding import PartitionSpec as P

F32 = jnp.float32
BF16 = jnp.bfloat16
MESH = pl.DeviceIdType.MESH
epsilon = 1e-05

X, K = 4, 2
SEQ = 8
TOK = 32
ROW = 16
HEADS = 8


def iota(shape, dim):
    return lax.broadcasted_iota(jnp.int32, shape, dim)


def one_hot(condition):
    return jnp.where(condition, 1.0, 0.0).astype(BF16)


def dot(a, b):
    return jnp.dot(a, b, preferred_element_type=F32)


def dot_nt(a, b, precision=None):
    return lax.dot_general(
        a, b, (((1,), (1,)), ((), ())), precision=precision, preferred_element_type=F32
    )


def normalized(source):
    center = source - jnp.mean(source, axis=-1, keepdims=True)
    spread = jnp.mean(center * center, axis=-1, keepdims=True)
    return center * lax.rsqrt(spread + epsilon)


def kernel(Y, Z, *refs):
    R = Y * X
    C = Z * K
    NS = R * SEQ
    NT = C * TOK
    hbm, (align_ref, pout_ref), refs = refs[:12], refs[12:14], refs[14:]
    local, refs = refs[:12], refs[12:]
    h_ref, pair_ref, seq_ref, tok_ref, pp_ref, mm_ref = local[:6]
    smt_ref, pay_ref, sw_ref, rett_ref, ti_ref, to_ref = local[6:]
    RB, LZ, LB, HB, EY, EX, MF, WB, AB, RT, VB, NB, MID, PNB = refs[:14]
    in_s, ry_s, rx_s, r_r, lz_s, lz_r, lx_s, l_r, lk_s, lk_r = refs[14:24]
    hz_s, hk_s, h_r, ez_s, ez_r, ex_s, ex_r = refs[24:]
    y, x = lax.axis_index("y"), lax.axis_index("x")
    z, k = lax.axis_index("z"), lax.axis_index("k")
    row = y * X + x
    col = z * K + k
    owner = k == x // 2
    far_first = sorted(range(1, Z), key=lambda t: -min(t, Z - t))
    near_first = far_first[::-1]

    def remote(src, dst, send, recv, **to):
        return pltpu.make_async_remote_copy(
            src_ref=src,
            dst_ref=dst,
            send_sem=send,
            recv_sem=recv,
            device_id=to,
            device_id_type=MESH,
        )

    barrier = pltpu.get_barrier_semaphore()
    for t in range(1, R):
        other = lax.rem(row + t, R)
        pl.semaphore_signal(
            barrier,
            inc=1,
            device_id={"y": other // X, "x": lax.rem(other, X)},
            device_id_type=MESH,
        )
    for t in range(1, C):
        other = lax.rem(col + t, C)
        pl.semaphore_signal(
            barrier,
            inc=1,
            device_id={"z": other // K, "k": lax.rem(other, K)},
            device_id_type=MESH,
        )

    def fetch(i):
        return pltpu.make_async_copy(hbm[i], local[i], in_s.at[i])

    for i in (0, 4, 3, 2, 5, 1, 6, 10, 11, 7, 8, 9):
        fetch(i).start()
    for i in (0, 4, 3, 2):
        fetch(i).wait()

    hf = h_ref[...].reshape(SEQ * TOK, 64).astype(F32)
    norm_f = normalized(hf)
    NB[...] = norm_f.astype(BF16)
    tokens = tok_ref[...].astype(F32)
    seqs = seq_ref[...].astype(F32)
    hit = iota((TOK, NT), 1) == col * TOK + iota((TOK, NT), 0)
    live_tok = jnp.sum(jnp.where(hit, tokens, 0.0), axis=1, keepdims=True)
    live_tok = jnp.concatenate([live_tok] * SEQ, axis=0)
    hit = iota((SEQ * TOK, NS), 1) == row * SEQ + iota((SEQ * TOK, NS), 0) // TOK
    live_seq = jnp.sum(jnp.where(hit, seqs, 0.0), axis=1, keepdims=True)
    inverse_count = 1.0 / jnp.maximum(jnp.sum(seqs, axis=1, keepdims=True), 1.0)
    norm = (norm_f * live_tok).astype(BF16)

    pp = pp_ref[...]
    mine = iota((256, 128), 0) % 4 == iota((256, 128), 1) // 32
    a, b = iota((64, 256), 0), iota((64, 256), 1)
    left_w = dot(pp, one_hot(iota((64, 128), 0) == iota((64, 128), 1) % 32)).astype(BF16)
    spread = dot(norm, left_w) * live_seq
    spread = jnp.where(mine, spread, 0.0).astype(BF16)
    pick = one_hot(
        (a % 8 == b // 32) & ((b % 32) // 4 == 4 * (a // 32) + 2 * ((a // 8) % 2) + (a // 16) % 2)
    )
    packed = dot(pick, spread).astype(BF16)
    for h in range(2):
        for t in range(2):
            LZ[z, h, :, t * 128 : (t + 1) * 128] = packed[(h * 2 + t) * 16 : (h * 2 + t + 1) * 16]

    right_t = dot_nt(one_hot(iota((32, 64), 1) == 32 + iota((32, 64), 0)), pp).astype(BF16)
    spread = []
    for s in range(SEQ):
        one = norm[s * TOK : (s + 1) * TOK]
        spread.append(dot_nt(right_t, jnp.concatenate([one] * 4, axis=0)))
    spread = jnp.concatenate(spread, axis=0)
    spread = jnp.where(mine, spread, 0.0).astype(BF16)
    pick = one_hot((a % 8 == b // 32) & ((b % 32) // 4 == ((a // 8) % 2) * 4 + a // 16))
    packed = dot(pick, spread).astype(BF16)
    for t in range(4):
        RB[row, :, t * 128 : (t + 1) * 128] = packed[t * 16 : (t + 1) * 16]

    u, v = iota((64, 128), 0), iota((64, 128), 1)
    HB[col] = (
        dot(norm[:128], one_hot(u == v)) + dot(norm[128:], one_hot(u + 64 == v))
    ).astype(BF16)

    pl.semaphore_wait(barrier, (R - 1) + (C - 1))

    def left_z(t):
        return remote(LZ.at[z], LZ.at[z], lz_s.at[t], lz_r.at[z], z=lax.rem(z + t, Z))

    def left_x(block, h):
        return remote(
            LZ.at[block, h],
            LB.at[row],
            lx_s.at[block, h],
            l_r.at[row],
            y=block,
            x=2 * k + h,
        )

    def left_here(block, h):
        return jnp.logical_and(block == y, 2 * k + h == x)

    def left_forward(block):
        for h in range(2):

            @pl.when(jnp.logical_not(left_here(block, h)))
            def _():
                left_x(block, h).start()

            @pl.when(left_here(block, h))
            def _():
                LB[row] = LZ[block, h]

    def left_k(block):
        part = pl.ds(block * X, X)
        return remote(LB.at[part], LB.at[part], lk_s.at[block], lk_r.at[block], k=1 - k)

    def right_y(t):
        return remote(RB.at[row], RB.at[row], ry_s.at[t], r_r.at[row], y=lax.rem(y + t, Y))

    def right_x(block, t):
        r = block * X + x
        return remote(
            RB.at[r], RB.at[r], rx_s.at[block, t], r_r.at[r], x=lax.rem(x + t, X)
        )

    def right_arrived(r):
        remote(RB.at[r], RB.at[r], ry_s.at[0], r_r.at[r], x=x).wait_recv()

    for t in far_first:
        left_z(t).start()
    for t in far_first:
        right_y(t).start()
    left_forward(z)
    for t in (2, 1, 3):
        right_x(y, t).start()

    fetch(5).wait()
    MF[...] = mm_ref[...].astype(F32)
    WB[...] = jnp.zeros_like(WB)
    for d in range(32):
        part = MF[pl.ds(d, 32, stride=32), :].astype(BF16)
        for i in range(4):
            WB[d * 128 + i * 32 : d * 128 + (i + 1) * 32, i * 128 : (i + 1) * 128] = part

    todo = list(near_first)
    for block in range(Y):

        @pl.when(block != y)
        def _():
            right_arrived(block * X + x)
            for t in (2, 1, 3):
                right_x(block, t).start()

        for t in todo[:2]:
            at = lax.rem(z + t, Z)
            remote(LZ.at[at], LZ.at[at], lz_s.at[0], lz_r.at[at], z=z).wait_recv()
            left_forward(at)
        todo = todo[2:]

    def hz(t):
        return remote(HB.at[col], HB.at[col], hz_s.at[t], h_r.at[col], z=lax.rem(z + t, Z))

    def hk(block):
        c = block * K + k
        return remote(HB.at[c], HB.at[c], hk_s.at[block], h_r.at[c], k=1 - k)

    def h_arrived(c):
        remote(HB.at[c], HB.at[c], hz_s.at[0], h_r.at[c], z=z).wait_recv()

    for t in far_first:
        hz(t).start()

    @pl.when(owner)
    def _():
        for block in range(Y):
            for other in range(X):
                r = block * X + other

                @pl.when(r != row)
                def _():
                    remote(LB.at[r], LB.at[r], lx_s.at[0, 0], l_r.at[r], x=x).wait_recv()

            left_k(block).start()

    for block in range(Y):
        for t in range(1, X):
            right_arrived(block * X + lax.rem(x + t, X))
    for half in range(2):
        right = RB[...].astype(F32).reshape(R, 2, SEQ, 512)[:, half].reshape(NS, 512)
        RT[half * 512 : (half + 1) * 512, :] = jnp.transpose(right).astype(BF16)

    @pl.when(jnp.logical_not(owner))
    def _():
        for block in range(Y):
            part = pl.ds(block * X, X)
            remote(LB.at[part], LB.at[part], lk_s.at[0], lk_r.at[block], y=y).wait_recv()

    left = LB[...].astype(F32).reshape(R, 2, SEQ, 256)
    left = jnp.concatenate(
        [left[:, 0].reshape(NS, 256), left[:, 1].reshape(NS, 256)], axis=1
    ).astype(BF16)
    for part in range(4):
        outer = dot(RT[part * 256 : (part + 1) * 256, :], left).astype(BF16)
        for dd in range(8):
            d = part * 8 + dd
            for g in range(4):
                AB[g * 32 : (g + 1) * 32, d * 128 : (d + 1) * 128] = outer[
                    dd * 32 : (dd + 1) * 32, g * 128 : (g + 1) * 128
                ]
    mean = dot(AB[...], WB[...]) * inverse_count
    mean = jnp.concatenate(
        [
            mean[(i // 4) * 32 : (i // 4 + 1) * 32, (i % 4) * 128 : (i % 4 + 1) * 128]
            for i in range(ROW)
        ],
        axis=0,
    )
    fetch(1).wait()
    fetch(6).wait()
    pair_mid = (pair_ref[...].reshape(ROW * TOK, 128).astype(F32) + mean).astype(BF16)
    MID[...] = pair_mid
    pair_norm = normalized(pair_mid.astype(F32))
    PNB[...] = pair_norm.astype(BF16)
    score_w = jnp.concatenate(
        [jnp.broadcast_to(smt_ref[h : h + 1, :], (ROW, 128)) for h in range(HEADS)], axis=0
    )
    every = dot_nt(pair_norm, score_w, lax.Precision.HIGHEST)
    lane_i = iota((TOK, 128), 1) % ROW
    scores = jnp.zeros((TOK, 128), F32)
    for i in range(ROW):
        scores = jnp.where(lane_i == i, every[i * TOK : (i + 1) * TOK], scores)
    shift = jnp.max(scores, axis=0, keepdims=True).astype(BF16).astype(F32)
    EY[0:TOK, :] = jnp.exp(scores - shift).astype(BF16)
    EY[TOK : TOK + 16, :] = jnp.broadcast_to(shift, (16, 128)).astype(BF16)

    def ez(to):
        return remote(
            EY, EX.at[x % 2, col], ez_s.at[to], ez_r.at[col], y=to, z=y, k=x // 2
        )

    def e_here(to):
        return jnp.logical_and(jnp.logical_and(to == y, z == y), owner)

    def ex(block, t):
        part = pl.ds(block * K, K)
        return remote(
            EX.at[x % 2, part],
            EX.at[x % 2, part],
            ex_s.at[block, t],
            ex_r.at[x % 2, block],
            x=lax.rem(x + t, X),
        )

    for to in range(Y):

        @pl.when(jnp.logical_not(e_here(to)))
        def _():
            ez(to).start()

        @pl.when(e_here(to))
        def _():
            EX[x % 2, col] = EY[...]

    hk(z).start()
    for t in near_first:
        block = lax.rem(z + t, Z)
        h_arrived(block * K + k)
        hk(block).start()
    fetch(10).wait()
    fetch(11).wait()
    for part in range(4):
        rows = slice(part * 128, (part + 1) * 128)
        pre = dot(PNB[rows, :], ti_ref[...])
        gate = pre[:, :512]
        hidden = (gate / (1.0 + jnp.exp(-gate)) * pre[:, 512:]).astype(BF16)
        out = (MID[rows, :].astype(F32) + dot(hidden, to_ref[...])).astype(BF16)
        pout_ref[part * 4 : (part + 1) * 4] = out.reshape(4, TOK, 128)

    @pl.when(owner)
    def _():
        for block in range(Z):
            for j in range(K):
                c = block * K + j

                @pl.when(jnp.logical_or(c != col, y != z))
                def _():
                    remote(EY, EX.at[x % 2, c], ez_s.at[0], ez_r.at[c], z=z).wait_recv()

            for t in (2, 1, 3):
                ex(block, t).start()

    for i in (7, 8, 9):
        fetch(i).wait()
    for t in range(Z):
        h_arrived(t * K + 1 - k)
    zeros = jnp.zeros((64, 256), BF16)
    for side in range(2):
        pay = jnp.concatenate(
            [pay_ref[...], zeros] if side == 0 else [zeros, pay_ref[...]], axis=0
        )
        for s in range(4):
            rows = HB[:, s * TOK : (s + 1) * TOK, :].reshape(NT, 128)
            VB[side * 4 + s] = dot(rows, pay).astype(BF16)
    gate = jax.nn.sigmoid(dot(NB[...], sw_ref[...]))

    weights = []
    for h in range(2):

        @pl.when(x != 2 * k + h)
        def _():
            for block in range(Z):
                part = pl.ds(block * K, K)
                remote(
                    EX.at[h, part], EX.at[h, part], ex_s.at[0, 0], ex_r.at[h, block], x=x
                ).wait_recv()

        shifts = EX[h, :, TOK : TOK + 16, :].astype(F32)[:, 0:1, :]
        factor = jnp.exp(shifts - jnp.max(shifts, axis=0, keepdims=True))
        w = EX[h, :, 0:TOK, :].astype(F32) * factor
        total = jnp.sum(jnp.sum(w, axis=0, keepdims=True), axis=1, keepdims=True)
        weights.append(jnp.transpose((w / total).reshape(NT, 128)).astype(BF16))
    weights = jnp.concatenate(weights, axis=0)
    head = iota((ROW, 256), 1) // 32
    averages = []
    for s in range(SEQ):
        full = dot(weights, VB[s])
        for half in range(2):
            average = jnp.zeros((ROW, 256), F32)
            for g in range(HEADS):
                start = half * 128 + g * ROW
                average = jnp.where(head == g, full[start : start + ROW], average)
            averages.append(average)
    gated = (gate * jnp.concatenate(averages, axis=0)).astype(BF16)
    out = h_ref[...].reshape(SEQ * TOK, 64).astype(F32) + dot_nt(gated, rett_ref[...])
    align_ref[...] = out.astype(BF16).reshape(SEQ, TOK, 64)

    for t in range(1, Y):
        right_y(t).wait_send()
    for block in range(Y):
        for t in range(1, X):
            right_x(block, t).wait_send()

        @pl.when(jnp.logical_not(e_here(block)))
        def _():
            ez(block).wait_send()

    for t in range(1, Z):
        left_z(t).wait_send()
        hz(t).wait_send()
    for block in range(Z):
        hk(block).wait_send()
        for h in range(2):

            @pl.when(jnp.logical_not(left_here(block, h)))
            def _():
                left_x(block, h).wait_send()

    @pl.when(owner)
    def _():
        for block in range(Y):
            left_k(block).wait_send()
        for block in range(Z):
            for t in range(1, X):
                ex(block, t).wait_send()


def body(h, pair, seq, tok, pp, mm, sm, pay, sw, ret, ti, to, *, Y, Z):
    R, C = Y * X, Z * K
    NT = C * TOK
    dma = pltpu.SemaphoreType.DMA
    args = (h, pair, seq.reshape(1, -1), tok.reshape(1, -1), pp, mm)
    args += (sm.T, pay, sw, ret.T, ti, to)
    return pl.pallas_call(
        functools.partial(kernel, Y, Z),
        out_shape=(
            jax.ShapeDtypeStruct(h.shape, BF16),
            jax.ShapeDtypeStruct(pair.shape, BF16),
        ),
        in_specs=[pl.BlockSpec(memory_space=pl.ANY)] * 12,
        out_specs=(pl.BlockSpec(memory_space=pltpu.VMEM),) * 2,
        scratch_shapes=[pltpu.VMEM(v.shape, v.dtype) for v in args]
        + [
            pltpu.VMEM((R, 16, 512), BF16),
            pltpu.VMEM((Z, 2, 16, 256), BF16),
            pltpu.VMEM((R, 16, 256), BF16),
            pltpu.VMEM((C, 128, 128), BF16),
            pltpu.VMEM((TOK + 16, 128), BF16),
            pltpu.VMEM((2, C, TOK + 16, 128), BF16),
            pltpu.VMEM((1024, 128), F32),
            pltpu.VMEM((4096, 512), BF16),
            pltpu.VMEM((128, 4096), BF16),
            pltpu.VMEM((1024, R * SEQ), BF16),
            pltpu.VMEM((SEQ, NT, 256), BF16),
            pltpu.VMEM((256, 64), BF16),
            pltpu.VMEM((512, 128), BF16),
            pltpu.VMEM((512, 128), BF16),
            dma((12,)),
            dma((Y,)),
            dma((Y, X)),
            dma((R,)),
            dma((Z,)),
            dma((Z,)),
            dma((Z, 2)),
            dma((R,)),
            dma((Y,)),
            dma((Y,)),
            dma((Z,)),
            dma((Z,)),
            dma((C,)),
            dma((Y,)),
            dma((C,)),
            dma((Z, X)),
            dma((2, Z)),
        ],
        compiler_params=pltpu.CompilerParams(
            collective_id=0, has_side_effects=True, vmem_limit_bytes=56 * 1024 * 1024
        ),
        cost_estimate=pl.CostEstimate(
            flops=3_000_000_000, bytes_accessed=2_000_000, transcendentals=400_000
        ),
    )(*args)


def solution(mesh):
    Y, Z = mesh.shape["row"] // X, mesh.shape["col"] // K
    split = Mesh(mesh.devices.reshape(Y, X, Z, K), ("y", "x", "z", "k"))
    tiled = P(("y", "x"), ("z", "k"), None)
    return jax.shard_map(
        functools.partial(body, Y=Y, Z=Z),
        mesh=split,
        in_specs=(tiled, tiled) + (P(),) * 10,
        out_specs=(tiled, tiled),
        check_vma=False,
    )
```

time: 60 us -> 48.6 us (0.81)
  the two profiles are of different devices: /device:TPU:64 before, /device:TPU:1 now
where the time goes in v2:
time: 48.6 us; the launch traced here: 47.6 us
  Pallas kernels  44.8 us (92%)
  local copies, waits for them, and re-layouts  2.17 us (4%)
  between operations  0.65 us (1%)
    pallas_call x1, Pallas kernels, body(): pl.pallas_call(functools.partial(kernel, Y, Z), out_shape=(jax.ShapeDtype...  44.8 us
    unnamed x4, local copies, waits for them, and re-layouts  2.17 us

profile of v2, /device:TPU:1, one launch (start us, length us, event | category | flops | bytes accessed | tf_op | source)
XLA Modules:
  0.0 47.6 jit_solution(5547204112165705399)
XLA Ops:
  0.6 44.8 %shard_map.131 = (bf16[8,32,64]{2,1,0:T(8,128)(2,1)}, bf16[16,32,128]{2,1,0:T(8,128)(2,1)}) custom-call(bf16[8,32,64]{2,1,0:T(8,128)(2,1)} %refs_0_.1, bf16[16,32,128]{2,1,0:T(8,128)(2,1)} %refs_1_.1, s32[1,256]{1,0:T(1,128)} %bitcast.7, s32[1,512]{1,0:T(1,128)} %bitcast.6, bf16[64,64]{1,0:T(8,128)(2,1)} %refs_4_.1, bf16[1024,128]{1,0:T(8,128)(2,1)} %refs_5_.1, ...), custom_call_target="tpu_custom_call" | custom-call | flops 3000000000 | bytes 2000000 | tf_op jit(solution)/shard_map/pallas_call | solution.py:436
  45.5 0.0 copy-start
  45.5 1.5 %copy.16 = bf16[8,32,64]{2,1,0:T(8,128)(2,1)} copy(bf16[8,32,64]{2,1,0:T(8,128)(2,1)} %get-tuple-element.4) | data formatting | bytes 65536
  47.0 0.0 copy-done
  47.0 0.7 %copy.17 = bf16[16,32,128]{2,1,0:T(8,128)(2,1)} copy(bf16[16,32,128]{2,1,0:T(8,128)(2,1)S(1)} %copy-done) | data formatting | bytes 262144
Async XLA Ops:
  45.5 1.5 %copy-start = (bf16[16,32,128]{2,1,0:T(8,128)(2,1)S(1)}, bf16[16,32,128]{2,1,0:T(8,128)(2,1)}, u32[]{:S(2)}) copy-start(bf16[16,32,128]{2,1,0:T(8,128)(2,1)} %get-tuple-element.5) | copy-start | bytes 393220

commit v3 on v2

--- a/solution.py
+++ b/solution.py
@@ -75,14 +75,11 @@
         )
 
     barrier = pltpu.get_barrier_semaphore()
-    for t in range(1, R):
-        other = lax.rem(row + t, R)
-        pl.semaphore_signal(
-            barrier,
-            inc=1,
-            device_id={"y": other // X, "x": lax.rem(other, X)},
-            device_id_type=MESH,
-        )
+    for axis, at, size in (("y", y, Y), ("x", x, X)):
+        for t in range(1, size):
+            pl.semaphore_signal(
+                barrier, inc=1, device_id={axis: lax.rem(at + t, size)}, device_id_type=MESH
+            )
     for t in range(1, C):
         other = lax.rem(col + t, C)
         pl.semaphore_signal(
@@ -139,12 +136,7 @@
     for t in range(4):
         RB[row, :, t * 128 : (t + 1) * 128] = packed[t * 16 : (t + 1) * 16]
 
-    u, v = iota((64, 128), 0), iota((64, 128), 1)
-    HB[col] = (
-        dot(norm[:128], one_hot(u == v)) + dot(norm[128:], one_hot(u + 64 == v))
-    ).astype(BF16)
-
-    pl.semaphore_wait(barrier, (R - 1) + (C - 1))
+    pl.semaphore_wait(barrier, (Y - 1) + (X - 1) + (C - 1))
 
     def left_z(t):
         return remote(LZ.at[z], LZ.at[z], lz_s.at[t], lz_r.at[z], z=lax.rem(z + t, Z))
@@ -193,9 +185,13 @@
         left_z(t).start()
     for t in far_first:
         right_y(t).start()
-    left_forward(z)
     for t in (2, 1, 3):
         right_x(y, t).start()
+
+    u, v = iota((64, 128), 0), iota((64, 128), 1)
+    HB[col] = (
+        dot(norm[:128], one_hot(u == v)) + dot(norm[128:], one_hot(u + 64 == v))
+    ).astype(BF16)
 
     fetch(5).wait()
     MF[...] = mm_ref[...].astype(F32)
@@ -205,20 +201,33 @@
         for i in range(4):
             WB[d * 128 + i * 32 : d * 128 + (i + 1) * 32, i * 128 : (i + 1) * 128] = part
 
-    todo = list(near_first)
-    for block in range(Y):
-
+    half = Y // 2
+    outer = jnp.logical_or(z < Y // 4, z >= Y - Y // 4)
+
+    def right_forward(block):
         @pl.when(block != y)
         def _():
             right_arrived(block * X + x)
             for t in (2, 1, 3):
                 right_x(block, t).start()
 
-        for t in todo[:2]:
-            at = lax.rem(z + t, Z)
-            remote(LZ.at[at], LZ.at[at], lz_s.at[0], lz_r.at[at], z=z).wait_recv()
-            left_forward(at)
-        todo = todo[2:]
+    def left_next(block):
+        @pl.when(block != z)
+        def _():
+            remote(
+                LZ.at[block], LZ.at[block], lz_s.at[0], lz_r.at[block], z=z
+            ).wait_recv()
+
+        left_forward(block)
+
+    for i in range(half):
+        right_forward(i)
+    for i in range(half):
+        left_next(jnp.where(outer, i, half - 1 - i))
+    for i in range(half, Y):
+        block = jnp.where(outer, Y + half - 1 - i, i)
+        right_forward(block)
+        left_next(block)
 
     def hz(t):
         return remote(HB.at[col], HB.at[col], hz_s.at[t], h_r.at[col], z=lax.rem(z + t, Z))
@@ -436,8 +445,8 @@
     return pl.pallas_call(
         functools.partial(kernel, Y, Z),
         out_shape=(
-            jax.ShapeDtypeStruct(h.shape, BF16),
-            jax.ShapeDtypeStruct(pair.shape, BF16),
+            pltpu.VMEM(h.shape, BF16),
+            pltpu.VMEM(pair.shape, BF16),
         ),
         in_specs=[pl.BlockSpec(memory_space=pl.ANY)] * 12,
         out_specs=(pl.BlockSpec(memory_space=pltpu.VMEM),) * 2,
@@ -476,7 +485,7 @@
             dma((2, Z)),
         ],
         compiler_params=pltpu.CompilerParams(
-            collective_id=0, has_side_effects=True, vmem_limit_bytes=56 * 1024 * 1024
+            collective_id=0, has_side_effects=True, vmem_limit_bytes=60 * 1024 * 1024
         ),
         cost_estimate=pl.CostEstimate(
             flops=3_000_000_000, bytes_accessed=2_000_000, transcendentals=400_000

time: 48.6 us -> 44.7 us (0.920)
  the two profiles are of different devices: /device:TPU:1 before, /device:TPU:120 now
where the time goes in v3:
time: 44.7 us; the launch traced here: 44.5 us
  Pallas kernels  42.6 us (95%)
  local copies, waits for them, and re-layouts  1.29 us (3%)
  between operations  0.64 us (1%)
    pallas_call x1, Pallas kernels, body(): pl.pallas_call(functools.partial(kernel, Y, Z), out_shape=(pltpu.VMEM(h.s...  42.6 us
    unnamed x2, local copies, waits for them, and re-layouts  1.29 us

profile of v3, /device:TPU:120, one launch (start us, length us, event | category | flops | bytes accessed | tf_op | source)
XLA Modules:
  0.0 44.5 jit_solution(8106788817516382131)
XLA Ops:
  0.6 42.6 %shard_map.131 = (bf16[8,32,64]{2,1,0:T(8,128)(2,1)S(1)}, bf16[16,32,128]{2,1,0:T(8,128)(2,1)S(1)}) custom-call(bf16[8,32,64]{2,1,0:T(8,128)(2,1)} %refs_0_.1, bf16[16,32,128]{2,1,0:T(8,128)(2,1)} %refs_1_.1, s32[1,256]{1,0:T(1,128)} %bitcast.7, s32[1,512]{1,0:T(1,128)} %bitcast.6, bf16[64,64]{1,0:T(8,128)(2,1)} %refs_4_.1, bf16[1024,128]{1,0:T(8,128)(2,1)} %refs_5_.1, ...), custom_call_target="tpu_custom_call" | custom-call | flops 3000000000 | bytes 2000000 | tf_op jit(solution)/shard_map/pallas_call | solution.py:445
  43.2 0.6 %copy.16 = bf16[8,32,64]{2,1,0:T(8,128)(2,1)} copy(bf16[8,32,64]{2,1,0:T(8,128)(2,1)S(1)} %get-tuple-element.2) | data formatting | bytes 65536
  43.9 0.7 %copy.17 = bf16[16,32,128]{2,1,0:T(8,128)(2,1)} copy(bf16[16,32,128]{2,1,0:T(8,128)(2,1)S(1)} %get-tuple-element.3) | data formatting | bytes 262144

commit v4 on v3

--- a/solution.py
+++ b/solution.py
@@ -53,9 +53,9 @@
     local, refs = refs[:12], refs[12:]
     h_ref, pair_ref, seq_ref, tok_ref, pp_ref, mm_ref = local[:6]
     smt_ref, pay_ref, sw_ref, rett_ref, ti_ref, to_ref = local[6:]
-    RB, LZ, LB, HB, EY, EX, MF, WB, AB, RT, VB, NB, MID, PNB = refs[:14]
-    in_s, ry_s, rx_s, r_r, lz_s, lz_r, lx_s, l_r, lk_s, lk_r = refs[14:24]
-    hz_s, hk_s, h_r, ez_s, ez_r, ex_s, ex_r = refs[24:]
+    RB, LZ, LB, HB, EY, EX, MF, WB, AB, RT, VB, NB, MID, PNB, GA, GB = refs[:16]
+    in_s, ry_s, rx_s, r_r, lz_s, lz_r, lx_s, l_r, lk_s, lk_r = refs[16:26]
+    hz_s, hk_s, h_r, ez_s, ez_r, ex_s, ex_r = refs[26:]
     y, x = lax.axis_index("y"), lax.axis_index("x")
     z, k = lax.axis_index("z"), lax.axis_index("k")
     row = y * X + x
@@ -75,19 +75,11 @@
         )
 
     barrier = pltpu.get_barrier_semaphore()
-    for axis, at, size in (("y", y, Y), ("x", x, X)):
+    for axis, at, size in (("y", y, Y), ("z", z, Z), ("x", x, X), ("k", k, K)):
         for t in range(1, size):
             pl.semaphore_signal(
                 barrier, inc=1, device_id={axis: lax.rem(at + t, size)}, device_id_type=MESH
             )
-    for t in range(1, C):
-        other = lax.rem(col + t, C)
-        pl.semaphore_signal(
-            barrier,
-            inc=1,
-            device_id={"z": other // K, "k": lax.rem(other, K)},
-            device_id_type=MESH,
-        )
 
     def fetch(i):
         return pltpu.make_async_copy(hbm[i], local[i], in_s.at[i])
@@ -136,7 +128,7 @@
     for t in range(4):
         RB[row, :, t * 128 : (t + 1) * 128] = packed[t * 16 : (t + 1) * 16]
 
-    pl.semaphore_wait(barrier, (Y - 1) + (X - 1) + (C - 1))
+    pl.semaphore_wait(barrier, (Y - 1) + (Z - 1) + (X - 1) + (K - 1))
 
     def left_z(t):
         return remote(LZ.at[z], LZ.at[z], lz_s.at[t], lz_r.at[z], z=lax.rem(z + t, Z))
@@ -224,23 +216,22 @@
         right_forward(i)
     for i in range(half):
         left_next(jnp.where(outer, i, half - 1 - i))
+    def hz(t):
+        return remote(HB.at[col], HB.at[col], hz_s.at[t], h_r.at[col], z=lax.rem(z + t, Z))
+
+    def hk(block):
+        c = block * K + k
+        return remote(HB.at[c], HB.at[c], hk_s.at[block], h_r.at[c], k=1 - k)
+
+    def h_arrived(c):
+        remote(HB.at[c], HB.at[c], hz_s.at[0], h_r.at[c], z=z).wait_recv()
+
+    for t in far_first:
+        hz(t).start()
     for i in range(half, Y):
         block = jnp.where(outer, Y + half - 1 - i, i)
         right_forward(block)
         left_next(block)
-
-    def hz(t):
-        return remote(HB.at[col], HB.at[col], hz_s.at[t], h_r.at[col], z=lax.rem(z + t, Z))
-
-    def hk(block):
-        c = block * K + k
-        return remote(HB.at[c], HB.at[c], hk_s.at[block], h_r.at[c], k=1 - k)
-
-    def h_arrived(c):
-        remote(HB.at[c], HB.at[c], hz_s.at[0], h_r.at[c], z=z).wait_recv()
-
-    for t in far_first:
-        hz(t).start()
 
     @pl.when(owner)
     def _():
@@ -373,10 +364,11 @@
         for s in range(4):
             rows = HB[:, s * TOK : (s + 1) * TOK, :].reshape(NT, 128)
             VB[side * 4 + s] = dot(rows, pay).astype(BF16)
-    gate = jax.nn.sigmoid(dot(NB[...], sw_ref[...]))
-
-    weights = []
-    for h in range(2):
+    GA[...] = jax.nn.sigmoid(dot(NB[...], sw_ref[...])).reshape(SEQ, 2, ROW, 256)
+
+    head = iota((ROW, 256), 1) // 32
+    for i in range(2):
+        h = lax.rem(x + i, 2)
 
         @pl.when(x != 2 * k + h)
         def _():
@@ -390,19 +382,14 @@
         factor = jnp.exp(shifts - jnp.max(shifts, axis=0, keepdims=True))
         w = EX[h, :, 0:TOK, :].astype(F32) * factor
         total = jnp.sum(jnp.sum(w, axis=0, keepdims=True), axis=1, keepdims=True)
-        weights.append(jnp.transpose((w / total).reshape(NT, 128)).astype(BF16))
-    weights = jnp.concatenate(weights, axis=0)
-    head = iota((ROW, 256), 1) // 32
-    averages = []
-    for s in range(SEQ):
-        full = dot(weights, VB[s])
-        for half in range(2):
+        weights = jnp.transpose((w / total).reshape(NT, 128)).astype(BF16)
+        for s in range(SEQ):
+            full = dot(weights, VB[s])
             average = jnp.zeros((ROW, 256), F32)
             for g in range(HEADS):
-                start = half * 128 + g * ROW
-                average = jnp.where(head == g, full[start : start + ROW], average)
-            averages.append(average)
-    gated = (gate * jnp.concatenate(averages, axis=0)).astype(BF16)
+                average = jnp.where(head == g, full[g * ROW : (g + 1) * ROW], average)
+            GB[s, h] = (GA[s, h] * average).astype(BF16)
+    gated = GB[...].reshape(SEQ * TOK, 256)
     out = h_ref[...].reshape(SEQ * TOK, 64).astype(F32) + dot_nt(gated, rett_ref[...])
     align_ref[...] = out.astype(BF16).reshape(SEQ, TOK, 64)
 
@@ -466,6 +453,8 @@
             pltpu.VMEM((256, 64), BF16),
             pltpu.VMEM((512, 128), BF16),
             pltpu.VMEM((512, 128), BF16),
+            pltpu.VMEM((SEQ, 2, ROW, 256), F32),
+            pltpu.VMEM((SEQ, 2, ROW, 256), BF16),
             dma((12,)),
             dma((Y,)),
             dma((Y, X)),

time: 44.7 us -> 43.6 us (0.975)
  the two profiles are of different devices: /device:TPU:120 before, /device:TPU:1 now
where the time goes in v4:
time: 43.6 us; the launch traced here: 43.5 us
  Pallas kernels  41.5 us (95%)
  local copies, waits for them, and re-layouts  1.29 us (3%)
  between operations  0.64 us (1%)
    pallas_call x1, Pallas kernels, body(): pl.pallas_call(functools.partial(kernel, Y, Z), out_shape=(pltpu.VMEM(h.s...  41.5 us
    unnamed x2, local copies, waits for them, and re-layouts  1.29 us

profile of v4, /device:TPU:1, one launch (start us, length us, event | category | flops | bytes accessed | tf_op | source)
XLA Modules:
  0.0 43.5 jit_solution(8294983099524709729)
XLA Ops:
  0.6 41.5 %shard_map.131 = (bf16[8,32,64]{2,1,0:T(8,128)(2,1)S(1)}, bf16[16,32,128]{2,1,0:T(8,128)(2,1)S(1)}) custom-call(bf16[8,32,64]{2,1,0:T(8,128)(2,1)} %refs_0_.1, bf16[16,32,128]{2,1,0:T(8,128)(2,1)} %refs_1_.1, s32[1,256]{1,0:T(1,128)} %bitcast.7, s32[1,512]{1,0:T(1,128)} %bitcast.6, bf16[64,64]{1,0:T(8,128)(2,1)} %refs_4_.1, bf16[1024,128]{1,0:T(8,128)(2,1)} %refs_5_.1, ...), custom_call_target="tpu_custom_call" | custom-call | flops 3000000000 | bytes 2000000 | tf_op jit(solution)/shard_map/pallas_call | solution.py:432
  42.2 0.6 %copy.16 = bf16[8,32,64]{2,1,0:T(8,128)(2,1)} copy(bf16[8,32,64]{2,1,0:T(8,128)(2,1)S(1)} %get-tuple-element.2) | data formatting | bytes 65536
  42.8 0.7 %copy.17 = bf16[16,32,128]{2,1,0:T(8,128)(2,1)} copy(bf16[16,32,128]{2,1,0:T(8,128)(2,1)S(1)} %get-tuple-element.3) | data formatting | bytes 262144

commit v5 on v4

--- a/solution.py
+++ b/solution.py
@@ -74,17 +74,24 @@
             device_id_type=MESH,
         )
 
-    barrier = pltpu.get_barrier_semaphore()
-    for axis, at, size in (("y", y, Y), ("z", z, Z), ("x", x, X), ("k", k, K)):
-        for t in range(1, size):
-            pl.semaphore_signal(
-                barrier, inc=1, device_id={axis: lax.rem(at + t, size)}, device_id_type=MESH
-            )
-
     def fetch(i):
         return pltpu.make_async_copy(hbm[i], local[i], in_s.at[i])
 
-    for i in (0, 4, 3, 2, 5, 1, 6, 10, 11, 7, 8, 9):
+    for i in (0, 4, 3, 2):
+        fetch(i).start()
+
+    barrier = pltpu.get_barrier_semaphore()
+    steps = [(axis, t) for axis, n in (("y", Y), ("z", Z), ("x", X), ("k", K)) for t in range(1, n)]
+    size, place = {"y": Y, "z": Z, "x": X, "k": K}, {"y": y, "z": z, "x": x, "k": k}
+    for axis, t in sorted(steps, key=lambda step: -min(step[1], size[step[0]] - step[1])):
+        pl.semaphore_signal(
+            barrier,
+            inc=1,
+            device_id={axis: lax.rem(place[axis] + t, size[axis])},
+            device_id_type=MESH,
+        )
+
+    for i in (5, 1, 6, 10, 11, 7, 8, 9):
         fetch(i).start()
     for i in (0, 4, 3, 2):
         fetch(i).wait()
@@ -339,6 +346,27 @@
         out = (MID[rows, :].astype(F32) + dot(hidden, to_ref[...])).astype(BF16)
         pout_ref[part * 4 : (part + 1) * 4] = out.reshape(4, TOK, 128)
 
+    for t in range(1, Y):
+        right_y(t).wait_send()
+    for block in range(Y):
+        for t in range(1, X):
+            right_x(block, t).wait_send()
+    for t in range(1, Z):
+        left_z(t).wait_send()
+        hz(t).wait_send()
+    for block in range(Z):
+        hk(block).wait_send()
+        for h in range(2):
+
+            @pl.when(jnp.logical_not(left_here(block, h)))
+            def _():
+                left_x(block, h).wait_send()
+
+    @pl.when(owner)
+    def _():
+        for block in range(Y):
+            left_k(block).wait_send()
+
     @pl.when(owner)
     def _():
         for block in range(Z):
@@ -393,34 +421,28 @@
     out = h_ref[...].reshape(SEQ * TOK, 64).astype(F32) + dot_nt(gated, rett_ref[...])
     align_ref[...] = out.astype(BF16).reshape(SEQ, TOK, 64)
 
-    for t in range(1, Y):
-        right_y(t).wait_send()
     for block in range(Y):
-        for t in range(1, X):
-            right_x(block, t).wait_send()
 
         @pl.when(jnp.logical_not(e_here(block)))
         def _():
             ez(block).wait_send()
 
-    for t in range(1, Z):
-        left_z(t).wait_send()
-        hz(t).wait_send()
-    for block in range(Z):
-        hk(block).wait_send()
-        for h in range(2):
-
-            @pl.when(jnp.logical_not(left_here(block, h)))
-            def _():
-                left_x(block, h).wait_send()
-
     @pl.when(owner)
     def _():
-        for block in range(Y):
-            left_k(block).wait_send()
         for block in range(Z):
             for t in range(1, X):
                 ex(block, t).wait_send()
+
+
+def place_outputs(align_ref, pout_ref, align_out, pair_out, sems):
+    copies = [
+        pltpu.make_async_copy(pout_ref, pair_out, sems.at[0]),
+        pltpu.make_async_copy(align_ref, align_out, sems.at[1]),
+    ]
+    for copy in copies:
+        copy.start()
+    for copy in copies:
+        copy.wait()
 
 
 def body(h, pair, seq, tok, pp, mm, sm, pay, sw, ret, ti, to, *, Y, Z):
@@ -429,7 +451,7 @@
     dma = pltpu.SemaphoreType.DMA
     args = (h, pair, seq.reshape(1, -1), tok.reshape(1, -1), pp, mm)
     args += (sm.T, pay, sw, ret.T, ti, to)
-    return pl.pallas_call(
+    align, out = pl.pallas_call(
         functools.partial(kernel, Y, Z),
         out_shape=(
             pltpu.VMEM(h.shape, BF16),
@@ -480,6 +502,16 @@
             flops=3_000_000_000, bytes_accessed=2_000_000, transcendentals=400_000
         ),
     )(*args)
+    return pl.pallas_call(
+        place_outputs,
+        out_shape=(pltpu.HBM(h.shape, BF16), pltpu.HBM(pair.shape, BF16)),
+        in_specs=[pl.BlockSpec(memory_space=pltpu.VMEM)] * 2,
+        out_specs=(pl.BlockSpec(memory_space=pltpu.HBM),) * 2,
+        scratch_shapes=[dma((2,))],
+    )(
+        pltpu.with_memory_space_constraint(align, pltpu.VMEM),
+        pltpu.with_memory_space_constraint(out, pltpu.VMEM),
+    )
 
 
 def solution(mesh):

time: 43.6 us -> 42.8 us (0.982)
  local copies, waits for them, and re-layouts: 1.29 us -> 0 us
  Pallas kernels: 41.5 us -> 42.1 us
    unnamed x2 -> x0, local copies, waits for them, and re-layouts: 1.29 us -> none
    pallas_call x0 -> x1, Pallas kernels: none -> 0.69 us  [body(): pl.pallas_call(place_outputs, out_shape=(pltpu.HBM(h.shape, BF16), pltpu....]
where the time goes in v5:
time: 42.8 us; the launch traced here: 42.7 us
  Pallas kernels  42.1 us (98%)
  between operations  0.64 us (1%)
    pallas_call x1, Pallas kernels, body(): pl.pallas_call(functools.partial(kernel, Y, Z), out_shape=(pltpu.VMEM(h.s...  41.4 us

profile of v5, /device:TPU:1, one launch (start us, length us, event | category | flops | bytes accessed | tf_op | source)
XLA Modules:
  0.0 42.7 jit_solution(7003008693229073270)
XLA Ops:
  0.6 41.4 %shard_map.131 = (bf16[8,32,64]{2,1,0:T(8,128)(2,1)S(1)}, bf16[16,32,128]{2,1,0:T(8,128)(2,1)S(1)}) custom-call(bf16[8,32,64]{2,1,0:T(8,128)(2,1)} %refs_0_.1, bf16[16,32,128]{2,1,0:T(8,128)(2,1)} %refs_1_.1, s32[1,256]{1,0:T(1,128)} %bitcast.7, s32[1,512]{1,0:T(1,128)} %bitcast.6, bf16[64,64]{1,0:T(8,128)(2,1)} %refs_4_.1, bf16[1024,128]{1,0:T(8,128)(2,1)} %refs_5_.1, ...), custom_call_target="tpu_custom_call" | custom-call | flops 3000000000 | bytes 2000000 | tf_op jit(solution)/shard_map/pallas_call | solution.py:454
  42.0 0.7 %shard_map.132 = (bf16[8,32,64]{2,1,0:T(8,128)(2,1)}, bf16[16,32,128]{2,1,0:T(8,128)(2,1)}) custom-call(bf16[8,32,64]{2,1,0:T(8,128)(2,1)S(1)} %get-tuple-element.4.align_ref, bf16[16,32,128]{2,1,0:T(8,128)(2,1)S(1)} %get-tuple-element.5.pout_ref), custom_call_target="tpu_custom_call" | custom-call | tf_op jit(solution)/shard_map/pallas_call | solution.py:505

commit v6 on v5

--- a/solution.py
+++ b/solution.py
@@ -182,7 +182,6 @@
 
     for t in far_first:
         left_z(t).start()
-    for t in far_first:
         right_y(t).start()
     for t in (2, 1, 3):
         right_x(y, t).start()
@@ -233,12 +232,13 @@
     def h_arrived(c):
         remote(HB.at[c], HB.at[c], hz_s.at[0], h_r.at[c], z=z).wait_recv()
 
-    for t in far_first:
-        hz(t).start()
     for i in range(half, Y):
         block = jnp.where(outer, Y + half - 1 - i, i)
         right_forward(block)
         left_next(block)
+
+    for t in far_first:
+        hz(t).start()
 
     @pl.when(owner)
     def _():

time: 42.8 us -> 42.8 us (level)
  no operation moved by 1% of the time
where the time goes in v6:
time: 42.8 us; the launch traced here: 42.7 us
  Pallas kernels  42 us (98%)
  between operations  0.64 us (1%)
    pallas_call x1, Pallas kernels, body(): pl.pallas_call(functools.partial(kernel, Y, Z), out_shape=(pltpu.VMEM(h.s...  41.3 us

profile of v6, /device:TPU:1, one launch (start us, length us, event | category | flops | bytes accessed | tf_op | source)
XLA Modules:
  0.0 42.7 jit_solution(10565970307978325180)
XLA Ops:
  0.6 41.3 %shard_map.131 = (bf16[8,32,64]{2,1,0:T(8,128)(2,1)S(1)}, bf16[16,32,128]{2,1,0:T(8,128)(2,1)S(1)}) custom-call(bf16[8,32,64]{2,1,0:T(8,128)(2,1)} %refs_0_.1, bf16[16,32,128]{2,1,0:T(8,128)(2,1)} %refs_1_.1, s32[1,256]{1,0:T(1,128)} %bitcast.7, s32[1,512]{1,0:T(1,128)} %bitcast.6, bf16[64,64]{1,0:T(8,128)(2,1)} %refs_4_.1, bf16[1024,128]{1,0:T(8,128)(2,1)} %refs_5_.1, ...), custom_call_target="tpu_custom_call" | custom-call | flops 3000000000 | bytes 2000000 | tf_op jit(solution)/shard_map/pallas_call | solution.py:454
  42.0 0.7 %shard_map.132 = (bf16[8,32,64]{2,1,0:T(8,128)(2,1)}, bf16[16,32,128]{2,1,0:T(8,128)(2,1)}) custom-call(bf16[8,32,64]{2,1,0:T(8,128)(2,1)S(1)} %get-tuple-element.4.align_ref, bf16[16,32,128]{2,1,0:T(8,128)(2,1)S(1)} %get-tuple-element.5.pout_ref), custom_call_target="tpu_custom_call" | custom-call | tf_op jit(solution)/shard_map/pallas_call | solution.py:505
